TPU v7x, 512 devices: a whole 4x8x8 slice. The times are simulated.
512 devices in a mesh: tile: 128 (over z, y, core), frame: 4 (over x).
Axes of the slice: x: 4, y: 8, z: 8, core: 2. Of those that a mesh axis runs over, the one named last changes fastest.
Arguments:
- recording: bfloat16 [131072, 512], P('tile', 'frame'), may hold values from 0 to 2
- footprints: bfloat16 [131072, 128], P('tile'), may hold values from 0 to 10, as said below
- slot_owner: int32 [16384, 1], P('tile'), may hold values from 0 to 127; in each aligned block of 128 rows (0 to 127, 128 to 255, ...) at most 2 rows name the same one
- slot_pick: int32 [16384], P('tile'), may hold values from 0 to 39
- traces: float32 [40960, 512], P('tile', 'frame'), may hold values from 0 to 1
Outputs:
- new_traces: float32 [40960, 512], P('tile', 'frame')
- new_footprints: bfloat16 [131072, 128], P('tile')
Inputs may be any that keep to these rules, and one draw needn't show every extreme that they name: `footprints`: nonnegative; a slot's nonzero entries mark its footprint's support, all other entries are exactly zero. `slot_owner`: of the 128 slots of one tile no owner is named by more than 2, a bound that some block reaches.
All inputs are finite; a program needn't handle non-finite values.
Results may differ from a plain program's by a relative error of at most 0.003.
Values may be sent and summed in bfloat16 or wider, within the bound.
A program may use at most 64 MiB of HBM per device.

v0:
```python
import jax
import jax.numpy as jnp
from jax import lax
from jax.sharding import PartitionSpec as P

ITER_C = 4
ITER_A = 8


def in_one_piece(arrays, axis, split_dim, concat_dim, along):
    widths = [a.shape[along] for a in arrays]
    both = jnp.concatenate(arrays, axis=along)
    whole = lax.all_to_all(both, axis, split_axis=split_dim, concat_axis=concat_dim, tiled=True)
    return tuple(jnp.split(whole, [sum(widths[:k]) for k in range(1, len(widths))], axis=along))


def side_by_side(arrays, axis, split_dim, concat_dim, along):
    columns = [a.reshape(*a.shape[:along], -1) for a in arrays]
    both = jnp.concatenate(columns, axis=along)
    whole, at, done = (
        lax.all_to_all(both, axis, split_axis=split_dim, concat_axis=concat_dim, tiled=True),
        0,
        [],
    )
    for a, column in zip(arrays, columns):
        piece = whole[..., at : at + column.shape[along]]
        done.append(piece.reshape(*piece.shape[:along], *a.shape[along:]))
        at += column.shape[along]
    return tuple(done)


def in_blocks(shard, dim, size):
    dims = shard.shape
    blocks = shard.reshape(*dims[:dim], size, dims[dim] // size, *dims[dim + 1 :])
    return jnp.moveaxis(blocks, dim, 0)


def sum_at_owner(shard, axis, dim):
    blocks = in_blocks(shard, dim, lax.axis_size(axis))
    arrived = lax.all_to_all(blocks, axis, split_axis=0, concat_axis=0, tiled=True)
    return arrived.sum(axis=0)


def sent_to_all(shard, axis):
    copies = jnp.broadcast_to(shard, (lax.axis_size(axis), *shard.shape))
    return lax.all_to_all(copies, axis, split_axis=0, concat_axis=0, tiled=True)


def over_copies(shard, axis):
    return sent_to_all(shard, axis).sum(axis=0)


def laid_out(blocks, dim):
    blocks = jnp.moveaxis(blocks, 0, dim)
    dims = blocks.shape
    return blocks.reshape(*dims[:dim], dims[dim] * dims[dim + 1], *dims[dim + 2 :])


def gathered_copies(shard, axis, dim):
    return laid_out(sent_to_all(shard, axis), dim)


def spread_rows(values, buffer_row, tile_count, capacity):
    filled = (
        jnp.zeros((tile_count * capacity,) + values.shape[1:], values.dtype)
        .at[buffer_row]
        .set(values)
    )
    return filled.reshape((tile_count, capacity) + values.shape[1:])


def body(recording, footprints, slot_owner, slot_pick, traces):
    tile_count = lax.axis_size("tile")
    slot_count = footprints.shape[1]
    owned_count = traces.shape[0]
    frame_count = traces.shape[1]
    capacity = max(2, 2 * slot_count // tile_count)
    buffer_size = tile_count * capacity
    owner_tile = slot_owner[:, 0]
    position = jnp.arange(slot_count, dtype=jnp.int32)
    earlier = (owner_tile[:, None] == owner_tile[None, :]) & (position[None, :] < position[:, None])
    slot_rank = jnp.sum(earlier.astype(jnp.int32), axis=1)
    buffer_row = owner_tile * capacity + slot_rank
    want_index = spread_rows(slot_pick, buffer_row, tile_count, capacity)
    want_valid = spread_rows(jnp.ones((slot_count,), jnp.int32), buffer_row, tile_count, capacity)
    got_index, got_valid = in_one_piece((want_index, want_valid), "tile", 0, 0, 1)
    owned_index = jnp.arange(owned_count, dtype=jnp.int32)
    select = (
        (got_index.reshape(-1)[:, None] == owned_index[None, :])
        & (got_valid.reshape(-1)[:, None] == 1)
    ).astype(jnp.float32)
    slot_gram = lax.dot_general(
        footprints, footprints, (((0,), (0,)), ((), ())), preferred_element_type=jnp.float32
    )
    data_drive = lax.dot_general(
        footprints, recording, (((0,), (0,)), ((), ())), preferred_element_type=jnp.float32
    )
    row_bound = jnp.sum(jnp.abs(slot_gram), axis=1)
    current = traces
    scale_row = jnp.ones((owned_count,), jnp.float32)
    slot_traces = traces[:slot_count]
    for iteration in range(ITER_C + 1):
        asked = jnp.dot(select, current, precision=lax.Precision.HIGHEST).reshape(
            tile_count, capacity, frame_count
        )
        arrived = lax.all_to_all(asked, "tile", split_axis=0, concat_axis=0, tiled=True)
        slot_traces = jnp.take(arrived.reshape(buffer_size, frame_count), buffer_row, axis=0)
        if iteration < ITER_C:
            slot_terms = (
                jnp.dot(slot_gram, slot_traces, precision=lax.Precision.HIGHEST) - data_drive
            )
            if iteration == 0:
                got_terms, got_bound = side_by_side(
                    (
                        spread_rows(slot_terms, buffer_row, tile_count, capacity),
                        spread_rows(row_bound, buffer_row, tile_count, capacity),
                    ),
                    "tile",
                    0,
                    0,
                    2,
                )
                bound_sum = jnp.dot(got_bound.reshape(-1), select, precision=lax.Precision.HIGHEST)
                scale_row = 1.0 / (1.0 + bound_sum)
            else:
                got_terms = lax.all_to_all(
                    spread_rows(slot_terms, buffer_row, tile_count, capacity),
                    "tile",
                    split_axis=0,
                    concat_axis=0,
                    tiled=True,
                )
            grad_sum = jnp.dot(
                select.T,
                got_terms.reshape(buffer_size, frame_count),
                precision=lax.Precision.HIGHEST,
            )
            current = jnp.maximum(current - grad_sum * scale_row[:, None], 0.0)
    slot_low = slot_traces.astype(jnp.bfloat16)
    data_term = lax.dot_general(
        recording, slot_low, (((1,), (1,)), ((), ())), preferred_element_type=jnp.float32
    )
    trace_term = jnp.dot(slot_traces, slot_traces.T, precision=lax.Precision.HIGHEST)
    data_sum = sum_at_owner(data_term, "frame", 0)
    trace_gram = over_copies(trace_term, "frame")
    share_rows = data_sum.shape[0]
    local_block = lax.dynamic_slice_in_dim(
        footprints, lax.axis_index("frame") * share_rows, share_rows, 0
    )
    column_step = 1.0 / (1.0 + jnp.sum(jnp.abs(trace_gram), axis=1))
    support = local_block > 0
    iterate = local_block.astype(jnp.float32)
    for sweep in range(ITER_A):
        moved = (
            iterate
            - (jnp.dot(iterate, trace_gram, precision=lax.Precision.HIGHEST) - data_sum)
            * column_step[None, :]
        )
        iterate = jnp.where(support, jnp.maximum(moved, 0.0), jnp.zeros_like(moved))
    updated = iterate.astype(jnp.bfloat16)
    updated = gathered_copies(updated, "frame", 0)
    return (current, updated)


def solution(mesh):
    in_specs = (P("tile", "frame"), P("tile", None), P("tile", None), P("tile"), P("tile", "frame"))
    out_specs = (P("tile", "frame"), P("tile", None))
    return jax.shard_map(body, mesh=mesh, in_specs=in_specs, out_specs=out_specs, check_vma=False)
```

profile of v0, /device:TPU:1, one launch (start us, length us, event | category | flops | bytes accessed | tf_op | source)
XLA Modules:
  0.0 246.3 jit_solution(16540844930288296812)
XLA Ops:
  0.7 0.7 copy-done.4
  1.5 1.0 scatter_custom_fusion.1
  2.7 1.1 scatter_custom_fusion
  3.9 0.7 pad_add_fusion
  4.6 18.4 %all-to-all-start = ((s32[128,1,4]{2,1,0:T(1,128)}), s32[128,1,4]{2,1,0:T(1,128)S(1)}, u32[]{:S(2)}, u32[]{:S(2)}) async-start(s32[128,1,4]{2,1,0:T(1,128)} %bitcast.4), calls=%async_computation | async-start | bytes 131072 | tf_op jit(solution)/shard_map/all_to_all | solution.py:13
  23.4 11.1 %all-to-all-done = s32[128,1,4]{2,1,0:T(1,128)S(1)} async-done(((s32[128,1,4]{2,1,0:T(1,128)}), s32[128,1,4]{2,1,0:T(1,128)S(1)}, u32[]{:S(2)}, u32[]{:S(2)}) %all-to-all-start) | async-done | bytes 2080 | tf_op jit(solution)/shard_map/all_to_all | solution.py:13
  34.8 1.1 fusion.55
  35.9 5.7 %all-to-all-start.1 = ((f32[128,2,128]{2,1,0:T(2,128)}), f32[128,2,128]{2,1,0:T(2,128)S(1)}, u32[]{:S(2)}, u32[]{:S(2)}) async-start(f32[128,2,128]{2,1,0:T(2,128)} %bitcast.6), calls=%async_computation.1 | async-start | bytes 262144 | tf_op jit(solution)/shard_map/all_to_all | solution.py:106
  41.7 1.0 scatter_custom_fusion.3
  43.2 11.3 %all-to-all-done.1 = f32[128,2,128]{2,1,0:T(2,128)S(1)} async-done(((f32[128,2,128]{2,1,0:T(2,128)}), f32[128,2,128]{2,1,0:T(2,128)S(1)}, u32[]{:S(2)}, u32[]{:S(2)}) %all-to-all-start.1) | async-done | bytes 131104 | tf_op jit(solution)/shard_map/all_to_all | solution.py:106
  54.5 0.6 gather_fusion
  55.1 0.3 convolution_subtract_fusion.11
  55.5 0.9 scatter_custom_fusion.2
  56.5 20.3 %all_to_all.72 = f32[128,2,129]{2,1,0:T(2,128)S(1)} all-to-all(f32[128,2,129]{2,1,0:T(2,128)S(1)} %pad_maximum_fusion), channel_id=1, replica_groups=mesh['tile'=128,'frame'=4] {'tile'}, dimensions={0} | all-to-all | bytes 264192 | tf_op jit(solution)/shard_map/all_to_all | solution.py:21
  77.1 0.3 convolution_reduce_fusion
  77.5 0.6 fusion.7
  78.2 0.4 fusion.51
  78.6 17.9 %all_to_all.73 = f32[128,2,128]{2,1,0:T(2,128)S(1)} all-to-all(f32[128,2,128]{2,1,0:T(2,128)S(1)} %bitcast.88), channel_id=1, replica_groups=mesh['tile'=128,'frame'=4] {'tile'}, dimensions={0} | all-to-all | bytes 262144 | tf_op jit(solution)/shard_map/all_to_all | solution.py:106
  96.5 0.6 gather_fusion.1
  97.1 0.3 convolution_subtract_fusion.10
  97.4 0.9 scatter_custom_fusion.4
  98.4 17.7 %all_to_all.74 = f32[128,2,128]{2,1,0:T(2,128)S(1)} all-to-all(f32[128,2,128]{2,1,0:T(2,128)S(1)} %bitcast.86), channel_id=1, replica_groups=mesh['tile'=128,'frame'=4] {'tile'}, dimensions={0} | all-to-all | bytes 262144 | tf_op jit(solution)/shard_map/all_to_all | solution.py:126
  116.1 0.6 fusion.5
  116.7 0.4 fusion.48
  117.1 17.8 %all_to_all.75 = f32[128,2,128]{2,1,0:T(2,128)S(1)} all-to-all(f32[128,2,128]{2,1,0:T(2,128)S(1)} %bitcast.89), channel_id=1, replica_groups=mesh['tile'=128,'frame'=4] {'tile'}, dimensions={0} | all-to-all | bytes 262144 | tf_op jit(solution)/shard_map/all_to_all | solution.py:106
  134.9 0.6 gather_fusion.2
  135.8 0.9 scatter_custom_fusion.5
  136.7 17.7 %all_to_all.76 = f32[128,2,128]{2,1,0:T(2,128)S(1)} all-to-all(f32[128,2,128]{2,1,0:T(2,128)S(1)} %bitcast.87), channel_id=1, replica_groups=mesh['tile'=128,'frame'=4] {'tile'}, dimensions={0} | all-to-all | bytes 262144 | tf_op jit(solution)/shard_map/all_to_all | solution.py:126
  154.5 0.6 fusion.3
  155.1 0.4 fusion.45
  155.5 17.8 %all_to_all.77 = f32[128,2,128]{2,1,0:T(2,128)S(1)} all-to-all(f32[128,2,128]{2,1,0:T(2,128)S(1)} %bitcast.90), channel_id=1, replica_groups=mesh['tile'=128,'frame'=4] {'tile'}, dimensions={0} | all-to-all | bytes 262144 | tf_op jit(solution)/shard_map/all_to_all | solution.py:106
  173.3 0.6 gather_fusion.3
  174.2 0.9 scatter_custom_fusion.6
  175.1 17.7 %all_to_all.78 = f32[128,2,128]{2,1,0:T(2,128)S(1)} all-to-all(f32[128,2,128]{2,1,0:T(2,128)S(1)} %bitcast.85), channel_id=1, replica_groups=mesh['tile'=128,'frame'=4] {'tile'}, dimensions={0} | all-to-all | bytes 262144 | tf_op jit(solution)/shard_map/all_to_all | solution.py:126
  192.9 0.6 fusion.1
  193.5 1.1 fusion.42
  194.6 5.6 %all-to-all-start.9 = ((f32[128,2,128]{2,1,0:T(2,128)}), f32[128,2,128]{2,1,0:T(2,128)S(1)}, u32[]{:S(2)}, u32[]{:S(2)}) async-start(f32[128,2,128]{2,1,0:T(2,128)} %bitcast.22), calls=%async_computation.9 | async-start | bytes 262144 | tf_op jit(solution)/shard_map/all_to_all | solution.py:106
  200.1 12.8 %all-to-all-done.9 = f32[128,2,128]{2,1,0:T(2,128)S(1)} async-done(((f32[128,2,128]{2,1,0:T(2,128)}), f32[128,2,128]{2,1,0:T(2,128)S(1)}, u32[]{:S(2)}, u32[]{:S(2)}) %all-to-all-start.9) | async-done | bytes 131104 | tf_op jit(solution)/shard_map/all_to_all | solution.py:106
  213.0 0.6 gather_fusion.4
  213.6 0.3 fusion.90
  214.0 0.7 broadcast_in_dim.19
  214.7 4.0 %all-to-all-start.10 = ((f32[4,128,128]{2,1,0:T(8,128)}), f32[4,128,128]{2,1,0:T(8,128)S(1)}, u32[]{:S(2)}, u32[]{:S(2)}) async-start(f32[4,128,128]{2,1,0:T(8,128)} %broadcast_in_dim.19), calls=%async_computation.10 | async-start | bytes 524288 | tf_op jit(solution)/shard_map/all_to_all | solution.py:46
  219.0 0.8 copy.41
  219.8 4.7 %all-to-all-done.10 = f32[4,128,128]{2,1,0:T(8,128)S(1)} async-done(((f32[4,128,128]{2,1,0:T(8,128)}), f32[4,128,128]{2,1,0:T(8,128)S(1)}, u32[]{:S(2)}, u32[]{:S(2)}) %all-to-all-start.10) | async-done | bytes 262176 | tf_op jit(solution)/shard_map/all_to_all | solution.py:46
  224.5 3.5 %all-to-all-start.11 = ((f32[4,256,128]{1,2,0:T(8,128)}), f32[4,256,128]{1,2,0:T(8,128)S(1)}, u32[]{:S(2)}, u32[]{:S(2)}) async-start(f32[4,256,128]{1,2,0:T(8,128)} %bitcast.70), calls=%async_computation.11 | async-start | bytes 1048576 | tf_op jit(solution)/shard_map/all_to_all | solution.py:40
  228.1 7.2 %all-to-all-done.11 = f32[4,256,128]{1,2,0:T(8,128)S(1)} async-done(((f32[4,256,128]{1,2,0:T(8,128)}), f32[4,256,128]{1,2,0:T(8,128)S(1)}, u32[]{:S(2)}, u32[]{:S(2)}) %all-to-all-start.11) | async-done | bytes 524320 | tf_op jit(solution)/shard_map/all_to_all | solution.py:40
  237.7 7.9 %all_to_all.79 = bf16[4,256,128]{2,1,0:T(8,128)(2,1)S(1)} all-to-all(bf16[4,256,128]{2,1,0:T(8,128)(2,1)S(1)} %broadcast_in_dim.20), channel_id=1, replica_groups=mesh['tile'=128,'frame'=4] {'frame'}, dimensions={0} | all-to-all | bytes 524288 | tf_op jit(solution)/shard_map/all_to_all | solution.py:46
  245.6 0.7 copy.52
  (45 shorter events, 5.6 us)
Async XLA Ops:
  0.6 42.3 %copy-start = (bf16[1024,128]{1,0:T(8,128)(2,1)S(1)}, bf16[1024,128]{1,0:T(8,128)(2,1)}, u32[]{:S(2)}) copy-start(bf16[1024,128]{1,0:T(8,128)(2,1)} %param.7) | copy-start | bytes 786436
  0.6 0.7 copy-start.4
  0.7 22.4 %copy-start.1 = (bf16[1024,128]{1,0:T(8,128)(2,1)S(1)}, bf16[1024,128]{1,0:T(8,128)(2,1)}, u32[]{:S(2)}) copy-start(bf16[1024,128]{1,0:T(8,128)(2,1)} %param.8) | copy-start | bytes 786436
  4.6 29.8 %all-to-all-start = ((s32[128,1,4]{2,1,0:T(1,128)}), s32[128,1,4]{2,1,0:T(1,128)S(1)}, u32[]{:S(2)}, u32[]{:S(2)}) async-start(s32[128,1,4]{2,1,0:T(1,128)} %bitcast.4), calls=%async_computation | async-start | bytes 131072 | tf_op jit(solution)/shard_map/all_to_all | solution.py:13
  23.4 11.5 %copy-start.2 = (f32[320,128]{1,0:T(8,128)S(1)}, f32[320,128]{1,0:T(8,128)}, u32[]{:S(2)}) copy-start(f32[320,128]{1,0:T(8,128)} %param.11) | copy-start | bytes 491524
  35.9 18.6 %all-to-all-start.1 = ((f32[128,2,128]{2,1,0:T(2,128)}), f32[128,2,128]{2,1,0:T(2,128)S(1)}, u32[]{:S(2)}, u32[]{:S(2)}) async-start(f32[128,2,128]{2,1,0:T(2,128)} %bitcast.6), calls=%async_computation.1 | async-start | bytes 262144 | tf_op jit(solution)/shard_map/all_to_all | solution.py:106
  193.5 1.1 copy-start.3
  194.6 18.4 %all-to-all-start.9 = ((f32[128,2,128]{2,1,0:T(2,128)}), f32[128,2,128]{2,1,0:T(2,128)S(1)}, u32[]{:S(2)}, u32[]{:S(2)}) async-start(f32[128,2,128]{2,1,0:T(2,128)} %bitcast.22), calls=%async_computation.9 | async-start | bytes 262144 | tf_op jit(solution)/shard_map/all_to_all | solution.py:106
  214.7 9.8 %all-to-all-start.10 = ((f32[4,128,128]{2,1,0:T(8,128)}), f32[4,128,128]{2,1,0:T(8,128)S(1)}, u32[]{:S(2)}, u32[]{:S(2)}) async-start(f32[4,128,128]{2,1,0:T(8,128)} %broadcast_in_dim.19), calls=%async_computation.10 | async-start | bytes 524288 | tf_op jit(solution)/shard_map/all_to_all | solution.py:46
  224.5 10.8 %all-to-all-start.11 = ((f32[4,256,128]{1,2,0:T(8,128)}), f32[4,256,128]{1,2,0:T(8,128)S(1)}, u32[]{:S(2)}, u32[]{:S(2)}) async-start(f32[4,256,128]{1,2,0:T(8,128)} %bitcast.70), calls=%async_computation.11 | async-start | bytes 1048576 | tf_op jit(solution)/shard_map/all_to_all | solution.py:40
where the time goes:
time: 249 us; the launch traced here: 246 us
  blocking collectives  135 us (54%)
  waiting for transfers between devices  47 us (19%)
  starting transfers between devices  37.2 us (15%)
  local copies, waits for them, and re-layouts  14.2 us (6%)
  matrix products  10.6 us (4%)
    all_to_all x3, blocking collectives, body(): lax.all_to_all(asked, 'tile', split_axis=0, concat_axis=0, tiled=True)  53.4 us
    all_to_all x3, blocking collectives, body(): lax.all_to_all(spread_rows(slot_terms, buffer_row, tile_count, capacity),...  53.2 us
    all_to_all x2, waiting for transfers between devices, body(): lax.all_to_all(asked, 'tile', split_axis=0, concat_axis=0, tiled=True)  24.1 us
    all_to_all x1, blocking collectives, side_by_side(): lax.all_to_all(both, axis, split_axis=split_dim, concat_axis=concat_dim,...  20.3 us
    all_to_all x1, starting transfers between devices, in_one_piece(): lax.all_to_all(both, axis, split_axis=split_dim, concat_axis=concat_dim,...  18.4 us
    all_to_all x2, starting transfers between devices, body(): lax.all_to_all(asked, 'tile', split_axis=0, concat_axis=0, tiled=True)  11.3 us
    all_to_all x1, waiting for transfers between devices, in_one_piece(): lax.all_to_all(both, axis, split_axis=split_dim, concat_axis=concat_dim,...  11.1 us
    all_to_all x1, blocking collectives, sent_to_all(): return lax.all_to_all(copies, axis, split_axis=0, concat_axis=0, tiled=True)  7.92 us
  transfers between devices with their start and end apart: 5, of which 5 were waited for; matrix products, arithmetic and copies ran while one was open for 1% of the time, Pallas kernels for 0%

commit v1 on v0

--- a/solution.py
+++ b/solution.py
@@ -1,6 +1,8 @@
 import jax
 import jax.numpy as jnp
 from jax import lax
+from jax.experimental import pallas as pl
+from jax.experimental.pallas import tpu as pltpu
 from jax.sharding import PartitionSpec as P
 
 ITER_C = 4
@@ -67,6 +69,46 @@
         .set(values)
     )
     return filled.reshape((tile_count, capacity) + values.shape[1:])
+
+
+MESH = pl.DeviceIdType.MESH
+
+
+def touch(x_ref, i_ref, o_ref, a, b, w, ss, rs):
+    me = lax.axis_index("tile")
+    fr = lax.axis_index("frame")
+    bar = pltpu.get_barrier_semaphore()
+    other = me + 1 - 2 * lax.rem(me, 2)
+    pl.semaphore_signal(bar, inc=1, device_id=(other, fr), device_id_type=MESH)
+    pl.semaphore_wait(bar, 1)
+    a[...] = x_ref[...]
+    h = pltpu.make_async_remote_copy(
+        src_ref=a.at[pl.ds(pl.multiple_of(lax.rem(me, 2) * 4, 4), 4)],
+        dst_ref=b.at[pl.ds(pl.multiple_of(lax.rem(me, 2) * 4, 4), 4)],
+        send_sem=ss, recv_sem=rs, device_id=(other, fr), device_id_type=MESH)
+    h.start()
+    h.wait()
+    v = a[pl.ds(0, 8, stride=4), :]
+    idx = i_ref[...]
+    g = jnp.take_along_axis(v, idx, axis=1)
+    k = jnp.take_along_axis(g, jnp.bitwise_and(idx, 7), axis=0)
+    t = jnp.transpose(jnp.concatenate([k] * 16, axis=0))
+    w[...] = t
+    w[pl.ds(0, 8, stride=4), :] = k
+    c = jnp.where(jnp.abs(jnp.sum(w[...])) < 0.0, 1.0, 0.0) + jnp.dot(t.astype(jnp.bfloat16), w[...].astype(jnp.bfloat16), preferred_element_type=jnp.float32) * 0.0
+    o_ref[...] = x_ref[...] + c[0:64, :] * 0.0
+
+
+def touched(x, i):
+    return pl.pallas_call(
+        touch,
+        out_shape=jax.ShapeDtypeStruct((64, 128), jnp.float32),
+        in_specs=[pl.BlockSpec(memory_space=pltpu.VMEM)] * 2,
+        out_specs=pl.BlockSpec(memory_space=pltpu.VMEM),
+        scratch_shapes=[pltpu.VMEM((64, 128), jnp.float32), pltpu.VMEM((64, 128), jnp.float32), pltpu.VMEM((128, 128), jnp.float32),
+                        pltpu.SemaphoreType.DMA, pltpu.SemaphoreType.DMA],
+        compiler_params=pltpu.CompilerParams(collective_id=0, has_side_effects=True, vmem_limit_bytes=30 << 20),
+    )(x, i)
 
 
 def body(recording, footprints, slot_owner, slot_pick, traces):
@@ -96,6 +138,8 @@
         footprints, recording, (((0,), (0,)), ((), ())), preferred_element_type=jnp.float32
     )
     row_bound = jnp.sum(jnp.abs(slot_gram), axis=1)
+    head = touched(traces[:64], jnp.broadcast_to(slot_pick[None, :], (8, 128)))
+    traces = jnp.concatenate([head, traces[64:]], axis=0)
     current = traces
     scale_row = jnp.ones((owned_count,), jnp.float32)
     slot_traces = traces[:slot_count]

time: 249 us -> 249 us (level)
  waiting for transfers between devices: 47 us -> 42.9 us
  Pallas kernels: 0 us -> 2.74 us
    all_to_all x1, waiting for transfers between devices: 11.1 us -> 7.02 us  [in_one_piece(): lax.all_to_all(both, axis, split_axis=split_dim, concat_axis=concat_dim,...]
    pallas_call x0 -> x1, Pallas kernels: none -> 2.74 us  [touched(): pl.pallas_call(touch, out_shape=jax.ShapeDtypeStruct((64, 128), jnp.float...]
  transfers between devices with their start and end apart: 5 -> 5, of which waited for: 5 -> 5; matrix products, arithmetic and copies ran while one was open for 1% -> 1% of each run, Pallas kernels for 0% -> 1%
where the time goes in v1:
time: 249 us; the launch traced here: 247 us
  blocking collectives  135 us (54%)
  waiting for transfers between devices  42.9 us (17%)
  starting transfers between devices  37.6 us (15%)
  local copies, waits for them, and re-layouts  15.5 us (6%)
  matrix products  10.6 us (4%)
  Pallas kernels  2.74 us (1%)
    all_to_all x3, blocking collectives, body(): lax.all_to_all(asked, 'tile', split_axis=0, concat_axis=0, tiled=True)  53.4 us
    all_to_all x3, blocking collectives, body(): lax.all_to_all(spread_rows(slot_terms, buffer_row, tile_count, capacity),...  53.3 us
    all_to_all x2, waiting for transfers between devices, body(): lax.all_to_all(asked, 'tile', split_axis=0, concat_axis=0, tiled=True)  24 us
    all_to_all x1, blocking collectives, side_by_side(): lax.all_to_all(both, axis, split_axis=split_dim, concat_axis=concat_dim,...  20.3 us
    all_to_all x1, starting transfers between devices, in_one_piece(): lax.all_to_all(both, axis, split_axis=split_dim, concat_axis=concat_dim,...  18.4 us
    all_to_all x2, starting transfers between devices, body(): lax.all_to_all(asked, 'tile', split_axis=0, concat_axis=0, tiled=True)  11.7 us
    all_to_all x1, blocking collectives, sent_to_all(): return lax.all_to_all(copies, axis, split_axis=0, concat_axis=0, tiled=True)  7.92 us
    all_to_all x1, waiting for transfers between devices, sum_at_owner(): lax.all_to_all(blocks, axis, split_axis=0, concat_axis=0, tiled=True)  7.14 us
  transfers between devices with their start and end apart: 5, of which 5 were waited for; matrix products, arithmetic and copies ran while one was open for 1% of the time, Pallas kernels for 1%

profile of v1, /device:TPU:1, one launch (start us, length us, event | category | flops | bytes accessed | tf_op | source)
XLA Modules:
  0.0 246.6 jit_solution(11239912539682640519)
XLA Ops:
  0.7 0.7 copy-done.5
  1.5 1.0 scatter_custom_fusion.1
  2.7 1.1 scatter_custom_fusion
  3.9 0.7 pad_add_fusion
  4.6 18.4 %all-to-all-start = ((s32[128,1,4]{2,1,0:T(1,128)}), s32[128,1,4]{2,1,0:T(1,128)S(1)}, u32[]{:S(2)}, u32[]{:S(2)}) async-start(s32[128,1,4]{2,1,0:T(1,128)} %bitcast.4), calls=%async_computation | async-start | bytes 131072 | tf_op jit(solution)/shard_map/all_to_all | solution.py:15
  23.4 0.6 copy-done.3
  24.0 0.6 copy-done.4
  24.7 2.7 %shard_map.68 = f32[64,128]{1,0:T(8,128)S(1)} custom-call(f32[64,128]{1,0:T(8,128)S(1)} %slice.12.x_ref, s32[8,128]{1,0:T(8,128)S(1)} %broadcast_in_dim.19.i_ref), custom_call_target="tpu_custom_call" | custom-call | tf_op jit(solution)/shard_map/pallas_call | solution.py:103
  27.4 7.0 %all-to-all-done = s32[128,1,4]{2,1,0:T(1,128)S(1)} async-done(((s32[128,1,4]{2,1,0:T(1,128)}), s32[128,1,4]{2,1,0:T(1,128)S(1)}, u32[]{:S(2)}, u32[]{:S(2)}) %all-to-all-start) | async-done | bytes 2080 | tf_op jit(solution)/shard_map/all_to_all | solution.py:15
  34.8 1.1 fusion.55
  35.9 6.2 %all-to-all-start.1 = ((f32[128,2,128]{2,1,0:T(2,128)}), f32[128,2,128]{2,1,0:T(2,128)S(1)}, u32[]{:S(2)}, u32[]{:S(2)}) async-start(f32[128,2,128]{2,1,0:T(2,128)} %bitcast.6), calls=%async_computation.1 | async-start | bytes 262144 | tf_op jit(solution)/shard_map/all_to_all | solution.py:150
  42.1 1.0 scatter_custom_fusion.3
  43.6 11.2 %all-to-all-done.1 = f32[128,2,128]{2,1,0:T(2,128)S(1)} async-done(((f32[128,2,128]{2,1,0:T(2,128)}), f32[128,2,128]{2,1,0:T(2,128)S(1)}, u32[]{:S(2)}, u32[]{:S(2)}) %all-to-all-start.1) | async-done | bytes 131104 | tf_op jit(solution)/shard_map/all_to_all | solution.py:150
  54.8 0.6 gather_fusion
  55.8 0.9 scatter_custom_fusion.2
  56.8 20.3 %all_to_all.72 = f32[128,2,129]{2,1,0:T(2,128)S(1)} all-to-all(f32[128,2,129]{2,1,0:T(2,128)S(1)} %pad_maximum_fusion), channel_id=1, replica_groups=mesh['tile'=128,'frame'=4] {'tile'}, dimensions={0} | all-to-all | bytes 264192 | tf_op jit(solution)/shard_map/all_to_all | solution.py:23
  77.8 0.6 fusion.7
  78.4 0.4 fusion.51
  78.9 17.9 %all_to_all.73 = f32[128,2,128]{2,1,0:T(2,128)S(1)} all-to-all(f32[128,2,128]{2,1,0:T(2,128)S(1)} %bitcast.86), channel_id=1, replica_groups=mesh['tile'=128,'frame'=4] {'tile'}, dimensions={0} | all-to-all | bytes 262144 | tf_op jit(solution)/shard_map/all_to_all | solution.py:150
  96.8 0.6 gather_fusion.1
  97.7 0.9 scatter_custom_fusion.4
  98.6 17.8 %all_to_all.74 = f32[128,2,128]{2,1,0:T(2,128)S(1)} all-to-all(f32[128,2,128]{2,1,0:T(2,128)S(1)} %bitcast.84), channel_id=1, replica_groups=mesh['tile'=128,'frame'=4] {'tile'}, dimensions={0} | all-to-all | bytes 262144 | tf_op jit(solution)/shard_map/all_to_all | solution.py:170
  116.4 0.6 fusion.5
  117.0 0.4 fusion.48
  117.4 17.7 %all_to_all.75 = f32[128,2,128]{2,1,0:T(2,128)S(1)} all-to-all(f32[128,2,128]{2,1,0:T(2,128)S(1)} %bitcast.87), channel_id=1, replica_groups=mesh['tile'=128,'frame'=4] {'tile'}, dimensions={0} | all-to-all | bytes 262144 | tf_op jit(solution)/shard_map/all_to_all | solution.py:150
  135.2 0.6 gather_fusion.2
  136.1 0.9 scatter_custom_fusion.5
  137.0 17.8 %all_to_all.76 = f32[128,2,128]{2,1,0:T(2,128)S(1)} all-to-all(f32[128,2,128]{2,1,0:T(2,128)S(1)} %bitcast.85), channel_id=1, replica_groups=mesh['tile'=128,'frame'=4] {'tile'}, dimensions={0} | all-to-all | bytes 262144 | tf_op jit(solution)/shard_map/all_to_all | solution.py:170
  154.8 0.6 fusion.3
  155.4 0.4 fusion.45
  155.8 17.8 %all_to_all.77 = f32[128,2,128]{2,1,0:T(2,128)S(1)} all-to-all(f32[128,2,128]{2,1,0:T(2,128)S(1)} %bitcast.88), channel_id=1, replica_groups=mesh['tile'=128,'frame'=4] {'tile'}, dimensions={0} | all-to-all | bytes 262144 | tf_op jit(solution)/shard_map/all_to_all | solution.py:150
  173.6 0.6 gather_fusion.3
  174.5 0.9 scatter_custom_fusion.6
  175.4 17.8 %all_to_all.78 = f32[128,2,128]{2,1,0:T(2,128)S(1)} all-to-all(f32[128,2,128]{2,1,0:T(2,128)S(1)} %bitcast.83), channel_id=1, replica_groups=mesh['tile'=128,'frame'=4] {'tile'}, dimensions={0} | all-to-all | bytes 262144 | tf_op jit(solution)/shard_map/all_to_all | solution.py:170
  193.2 0.6 fusion.1
  193.8 1.1 fusion.42
  194.9 5.6 %all-to-all-start.9 = ((f32[128,2,128]{2,1,0:T(2,128)}), f32[128,2,128]{2,1,0:T(2,128)S(1)}, u32[]{:S(2)}, u32[]{:S(2)}) async-start(f32[128,2,128]{2,1,0:T(2,128)} %bitcast.22), calls=%async_computation.9 | async-start | bytes 262144 | tf_op jit(solution)/shard_map/all_to_all | solution.py:150
  200.4 12.8 %all-to-all-done.9 = f32[128,2,128]{2,1,0:T(2,128)S(1)} async-done(((f32[128,2,128]{2,1,0:T(2,128)}), f32[128,2,128]{2,1,0:T(2,128)S(1)}, u32[]{:S(2)}, u32[]{:S(2)}) %all-to-all-start.9) | async-done | bytes 131104 | tf_op jit(solution)/shard_map/all_to_all | solution.py:150
  213.3 0.6 gather_fusion.4
  213.9 0.3 fusion.90
  214.3 0.7 broadcast_in_dim.22
  215.0 4.0 %all-to-all-start.10 = ((f32[4,128,128]{2,1,0:T(8,128)}), f32[4,128,128]{2,1,0:T(8,128)S(1)}, u32[]{:S(2)}, u32[]{:S(2)}) async-start(f32[4,128,128]{2,1,0:T(8,128)} %broadcast_in_dim.22), calls=%async_computation.10 | async-start | bytes 524288 | tf_op jit(solution)/shard_map/all_to_all | solution.py:48
  219.3 0.8 copy.41
  220.1 4.7 %all-to-all-done.10 = f32[4,128,128]{2,1,0:T(8,128)S(1)} async-done(((f32[4,128,128]{2,1,0:T(8,128)}), f32[4,128,128]{2,1,0:T(8,128)S(1)}, u32[]{:S(2)}, u32[]{:S(2)}) %all-to-all-start.10) | async-done | bytes 262176 | tf_op jit(solution)/shard_map/all_to_all | solution.py:48
  224.8 3.5 %all-to-all-start.11 = ((f32[4,256,128]{1,2,0:T(8,128)}), f32[4,256,128]{1,2,0:T(8,128)S(1)}, u32[]{:S(2)}, u32[]{:S(2)}) async-start(f32[4,256,128]{1,2,0:T(8,128)} %bitcast.69), calls=%async_computation.11 | async-start | bytes 1048576 | tf_op jit(solution)/shard_map/all_to_all | solution.py:42
  228.4 7.1 %all-to-all-done.11 = f32[4,256,128]{1,2,0:T(8,128)S(1)} async-done(((f32[4,256,128]{1,2,0:T(8,128)}), f32[4,256,128]{1,2,0:T(8,128)S(1)}, u32[]{:S(2)}, u32[]{:S(2)}) %all-to-all-start.11) | async-done | bytes 524320 | tf_op jit(solution)/shard_map/all_to_all | solution.py:42
  238.0 7.9 %all_to_all.79 = bf16[4,256,128]{2,1,0:T(8,128)(2,1)S(1)} all-to-all(bf16[4,256,128]{2,1,0:T(8,128)(2,1)S(1)} %broadcast_in_dim.23), channel_id=1, replica_groups=mesh['tile'=128,'frame'=4] {'frame'}, dimensions={0} | all-to-all | bytes 524288 | tf_op jit(solution)/shard_map/all_to_all | solution.py:48
  245.9 0.7 copy.52
  (51 shorter events, 6.6 us)
Async XLA Ops:
  0.6 42.7 %copy-start = (bf16[1024,128]{1,0:T(8,128)(2,1)S(1)}, bf16[1024,128]{1,0:T(8,128)(2,1)}, u32[]{:S(2)}) copy-start(bf16[1024,128]{1,0:T(8,128)(2,1)} %param.7) | copy-start | bytes 786436
  0.6 0.7 copy-start.5
  0.7 22.4 %copy-start.1 = (bf16[1024,128]{1,0:T(8,128)(2,1)S(1)}, bf16[1024,128]{1,0:T(8,128)(2,1)}, u32[]{:S(2)}) copy-start(bf16[1024,128]{1,0:T(8,128)(2,1)} %param.8) | copy-start | bytes 786436
  4.6 29.8 %all-to-all-start = ((s32[128,1,4]{2,1,0:T(1,128)}), s32[128,1,4]{2,1,0:T(1,128)S(1)}, u32[]{:S(2)}, u32[]{:S(2)}) async-start(s32[128,1,4]{2,1,0:T(1,128)} %bitcast.4), calls=%async_computation | async-start | bytes 131072 | tf_op jit(solution)/shard_map/all_to_all | solution.py:15
  23.1 0.9 copy-start.3
  24.0 0.7 copy-start.4
  35.9 18.9 %all-to-all-start.1 = ((f32[128,2,128]{2,1,0:T(2,128)}), f32[128,2,128]{2,1,0:T(2,128)S(1)}, u32[]{:S(2)}, u32[]{:S(2)}) async-start(f32[128,2,128]{2,1,0:T(2,128)} %bitcast.6), calls=%async_computation.1 | async-start | bytes 262144 | tf_op jit(solution)/shard_map/all_to_all | solution.py:150
  193.8 1.1 copy-start.2
  194.9 18.4 %all-to-all-start.9 = ((f32[128,2,128]{2,1,0:T(2,128)}), f32[128,2,128]{2,1,0:T(2,128)S(1)}, u32[]{:S(2)}, u32[]{:S(2)}) async-start(f32[128,2,128]{2,1,0:T(2,128)} %bitcast.22), calls=%async_computation.9 | async-start | bytes 262144 | tf_op jit(solution)/shard_map/all_to_all | solution.py:150
  215.0 9.8 %all-to-all-start.10 = ((f32[4,128,128]{2,1,0:T(8,128)}), f32[4,128,128]{2,1,0:T(8,128)S(1)}, u32[]{:S(2)}, u32[]{:S(2)}) async-start(f32[4,128,128]{2,1,0:T(8,128)} %broadcast_in_dim.22), calls=%async_computation.10 | async-start | bytes 524288 | tf_op jit(solution)/shard_map/all_to_all | solution.py:48
  224.8 10.8 %all-to-all-start.11 = ((f32[4,256,128]{1,2,0:T(8,128)}), f32[4,256,128]{1,2,0:T(8,128)S(1)}, u32[]{:S(2)}, u32[]{:S(2)}) async-start(f32[4,256,128]{1,2,0:T(8,128)} %bitcast.69), calls=%async_computation.11 | async-start | bytes 1048576 | tf_op jit(solution)/shard_map/all_to_all | solution.py:42

commit v2 on v0

v2 whole, which is shorter than its diff:
```python
import jax
import jax.numpy as jnp
from jax import lax
from jax.experimental import pallas as pl
from jax.experimental.pallas import tpu as pltpu
from jax.sharding import PartitionSpec as P

ITER_C = 4
ITER_A = 8
RING = 8
CHIPS = 64
XS = 4
PICKS = 40
K = 128
V = 1024
MESH = pl.DeviceIdType.MESH
F32 = jnp.float32
BF16 = jnp.bfloat16
I32 = jnp.int32


def dot(a, b):
    return jnp.dot(a, b, preferred_element_type=F32)


def dot_t(a, b):
    return lax.dot_general(a, b, (((0,), (0,)), ((), ())), preferred_element_type=F32)


def split(v):
    hi = v.astype(BF16)
    return hi, (v - hi.astype(F32)).astype(BF16)


def remote(src, dst, send, recv, tile, frame):
    return pltpu.make_async_remote_copy(
        src_ref=src, dst_ref=dst, send_sem=send, recv_sem=recv, device_id=(tile, frame), device_id_type=MESH
    )


def drain(ref, sem):
    pltpu.make_async_copy(ref, ref, sem).wait()


def ring_order(i):
    half = (i + 1) // 2
    return lax.rem(RING + half * (2 * (i % 2) - 1), RING)


def pick_rows(table, row, pick):
    low, high = jnp.bitwise_and(pick, 7), pick >> 3
    out = jnp.zeros(pick.shape, F32)
    for j in range(PICKS // 8):
        got = jnp.take_along_axis(table[row + 8 * j : row + 8 * j + 8, :], low, axis=0)
        out = jnp.where(high == j, got, out)
    return out


def kernel(
    rec, foot, owner_in, pick_in, traces,
    out_traces, out_foot,
    grams, msg, got, half, part, part_in, bound_in, table, scale, s_buf, back, back_in, s_all, y_all, x_buf, q_buf, a_buf, w_buf,
    pick_s, slot_s, lane_s, rank_s, turn,
    gram_send, gram_one, gram_two, msg_send, msg_recv, core_send, core_recv, back_send, back_recv, x_send, x_recv, y_send, y_recv, here_sem,
):
    me = lax.axis_index("tile")
    x = lax.axis_index("frame")
    c = lax.rem(me, 2)
    q = me // 2
    zc, yc = q // RING, lax.rem(q, RING)
    sibling = me + 1 - 2 * c
    a = zc * (1 - c) + yc * c
    b = yc * (1 - c) + zc * c
    sa, sb = RING - (RING - 1) * c, 1 + (RING - 1) * c

    barrier = pltpu.get_barrier_semaphore()

    def greet(i, carry):
        pl.semaphore_signal(barrier, inc=1, device_id=(lax.rem(q + i, CHIPS) * 2 + c, x), device_id_type=MESH)
        return carry

    lax.fori_loop(1, CHIPS, greet, 0)
    pl.semaphore_signal(barrier, inc=1, device_id=(sibling, x), device_id_type=MESH)
    for i in range(1, XS):
        pl.semaphore_signal(barrier, inc=1, device_id=(me, lax.rem(x + i, XS)), device_id_type=MESH)

    block = foot[...]
    gram = dot_t(block, block)
    drive = dot_t(rec[...], block)
    grams[q] = gram.astype(BF16)
    bound = jnp.sum(jnp.abs(gram), axis=0, keepdims=True)
    lane = lax.broadcasted_iota(I32, (K, K), 1)
    sub = lax.broadcasted_iota(I32, (K, K), 0)
    own = owner_in[...]
    own = jnp.broadcast_to((own & 1) * CHIPS + (own >> 1), (K, K))
    own_t = jnp.transpose(own.astype(F32)).astype(I32)
    pick_t = jnp.transpose(jnp.broadcast_to(pick_in[...], (K, K)).astype(F32)).astype(I32)
    same = own == own_t
    rank_row = jnp.sum(jnp.where(same & (sub < lane), 1.0, 0.0), axis=0, keepdims=True)
    rank_col = jnp.sum(jnp.where(same & (lane < sub), 1.0, 0.0), axis=1, keepdims=True)
    code = (pick_t * K + sub + 1).astype(F32)
    here = own_t == lane
    code0 = jnp.sum(jnp.where(here & (rank_col < 0.5), code, 0.0), axis=0, keepdims=True)
    code1 = jnp.sum(jnp.where(here & (rank_col > 0.5), code, 0.0), axis=0, keepdims=True)
    slot_code = own[0:1, :].astype(F32) * 2.0 + rank_row
    by_frame = jnp.transpose(traces[0:K, :])
    low_lane = lax.broadcasted_iota(I32, (CHIPS, K), 1) < CHIPS
    rows = (
        drive[0:CHIPS],
        drive[CHIPS:K],
        jnp.where(low_lane, by_frame[0:CHIPS], pltpu.roll(by_frame[CHIPS:K], CHIPS, 1)),
        jnp.broadcast_to(code0, (CHIPS, K)),
        jnp.broadcast_to(code1, (CHIPS, K)),
        jnp.broadcast_to(slot_code, (CHIPS, K)),
        jnp.broadcast_to(bound, (CHIPS, K)),
        jnp.zeros((CHIPS, K), F32),
    )
    for j, row in enumerate(rows):
        msg[pl.ds(j, CHIPS, stride=8), :] = row
    got[pl.ds(pl.multiple_of(q * 8, 8), 8), :] = msg[pl.ds(pl.multiple_of(q * 8, 8), 8), :]

    pl.semaphore_wait(barrier, CHIPS - 1 + 1 + XS - 1)

    up = (a * sa + lax.rem(b + 1, RING) * sb) * 2 + c
    down = (a * sa + lax.rem(b + RING - 1, RING) * sb) * 2 + c

    def forward(step, i, off, want_up, want_down):
        r = ring_order(i)
        column = lax.rem(a + r, RING) * sa
        if want_up:
            p = column + lax.rem(b + RING - off, RING) * sb
            remote(grams.at[p], grams.at[p], gram_send, gram_two.at[step, 0, i], up, x).start()
        if want_down:
            p = column + lax.rem(b + off, RING) * sb
            remote(grams.at[p], grams.at[p], gram_send, gram_two.at[step, 1, i], down, x).start()

    forward(0, 0, 0, True, True)

    def first(i, carry):
        r = ring_order(i)
        peer = (lax.rem(a + RING - r, RING) * sa + b * sb) * 2 + c
        remote(grams.at[q], grams.at[q], gram_send, gram_one.at[i], peer, x).start()
        return carry

    lax.fori_loop(1, RING, first, 0)

    def tell(i, carry):
        p = lax.rem(q + i, CHIPS)
        remote(
            msg.at[pl.ds(pl.multiple_of(p * 8, 8), 8)],
            got.at[pl.ds(pl.multiple_of(q * 8, 8), 8)],
            msg_send, msg_recv, p * 2 + c, x,
        ).start()
        return carry

    lax.fori_loop(1, CHIPS, tell, 0)
    for i in range(1, XS):
        remote(rec, y_all.at[x], y_send.at[i], y_recv.at[i], me, lax.rem(x + i, XS)).start()
    y_own = pltpu.make_async_copy(rec, y_all.at[x], here_sem.at[0])
    y_own.start()

    def pass_on(i, carry):
        pltpu.make_async_copy(grams.at[0], grams.at[0], gram_one.at[i]).wait()
        forward(0, i, 0, True, True)
        return carry

    lax.fori_loop(1, RING, pass_on, 0)

    def arrived(step, side, i):
        pltpu.make_async_copy(grams.at[0], grams.at[0], gram_two.at[step, side, i]).wait()

    for step in range(1, 3):

        def hop(i, carry, step=step):
            arrived(step - 1, 0, i)
            arrived(step - 1, 1, i)
            forward(step, i, step, True, True)
            return carry

        lax.fori_loop(0, RING, hop, 0)

    def last_up(i, carry):
        arrived(2, 0, i)
        arrived(2, 1, i)
        forward(3, i, 3, True, False)
        return carry

    def last_down(i, carry):
        arrived(2, 0, i)
        arrived(2, 1, i)
        forward(3, i, 3, False, True)
        return carry

    lax.fori_loop(0, RING // 2, last_up, 0)
    lax.fori_loop(RING // 2, RING, last_down, 0)

    drain(got.at[pl.ds(0, (CHIPS - 1) * 8)], msg_recv)
    half[c] = got[pl.ds(2, CHIPS, stride=8), :]
    swap = remote(half.at[c], half.at[c], core_send.at[0], core_recv.at[0], sibling, x)
    swap.start()
    for r in range(2):
        m = got[pl.ds(3 + r, CHIPS, stride=8), :].astype(I32) - 1
        pick_s[r] = m >> 7
        slot_s[r] = m & (K - 1)
    m = got[pl.ds(5, CHIPS, stride=8), :].astype(I32)
    lane_s[...] = m >> 1
    rank_s[...] = m & 1

    def scatter(n, into):
        def eight(j, carry):
            base = pl.multiple_of(j * 8, 8)
            sums = [[jnp.zeros((8, K), F32) for _ in range(8)] for _ in range(n)]
            for r in range(2):
                for g in range(CHIPS // 8):
                    p = pick_s[r, 8 * g : 8 * g + 8, :] - base
                    vals = [turn[r, f, 8 * g : 8 * g + 8, :] for f in range(n)]
                    for k in range(8):
                        hit = p == k
                        for f in range(n):
                            sums[f][k] = sums[f][k] + jnp.where(hit, vals[f], 0.0)
            for f in range(n):
                done = [jnp.sum(sums[f][k], axis=0, keepdims=True) for k in range(8)]
                into[pl.ds(pl.multiple_of(base + f * PICKS, 8), 8), :] = jnp.concatenate(done, axis=0)
            return carry

        lax.fori_loop(0, PICKS // 8, eight, 0)

    for g in range(CHIPS // 8):
        s8 = slice(8 * g, 8 * g + 8)
        vals = got[pl.ds(64 * g + 6, 8, stride=8), :]
        for r in range(2):
            turn[r, 0, s8, :] = jnp.take_along_axis(vals, slot_s[r, s8, :], axis=1)
    scatter(1, part.at[0])
    bound_swap = remote(
        part.at[0, pl.ds(0, PICKS)], bound_in, core_send.at[1], core_recv.at[1], sibling, x
    )
    bound_swap.start()
    swap.wait()
    table[...] = jnp.transpose(jnp.concatenate([half[0], half[1]], axis=0))
    bound_swap.wait()
    scale[...] = 1.0 / (1.0 + (part[0, 0:PICKS, :] + bound_in[...]))

    def gathered(f, g):
        s8 = slice(8 * g, 8 * g + 8)
        lanes = lane_s[s8, :]
        first_rank = jnp.take_along_axis(pick_rows(table, f * CHIPS, pick_s[0, s8, :]), lanes, axis=1)
        second_rank = jnp.take_along_axis(pick_rows(table, f * CHIPS, pick_s[1, s8, :]), lanes, axis=1)
        return jnp.where(rank_s[s8, :] == 0, first_rank, second_rank)

    for i in range(4):
        def last(k, carry, i=i):
            arrived(3, i // 2, k)
            return carry
        if i == 0:
            lax.fori_loop(0, RING // 2, last, 0)
        if i == 2:
            lax.fori_loop(RING // 2, RING, last, 0)

    sub8 = lax.broadcasted_iota(I32, (8, K), 0)

    def sweep(it, carry):
        for g in range(CHIPS // 8):
            s8 = slice(8 * g, 8 * g + 8)
            h0, l0 = split(gathered(0, g))
            h1, l1 = split(gathered(1, g))
            left = jnp.concatenate([h0, l0, h1, l1], axis=0)
            g0 = -got[pl.ds(64 * g, 8, stride=8), :]
            g1 = -got[pl.ds(64 * g + 1, 8, stride=8), :]
            for j in range(8):
                m = dot(left, grams[8 * g + j])
                g0 = g0 + jnp.where(sub8 == j, m[0:8] + m[8:16], 0.0)
                g1 = g1 + jnp.where(sub8 == j, m[16:24] + m[24:32], 0.0)
            for r in range(2):
                slots = slot_s[r, s8, :]
                turn[r, 0, s8, :] = jnp.take_along_axis(g0, slots, axis=1)
                turn[r, 1, s8, :] = jnp.take_along_axis(g1, slots, axis=1)
        mine = part.at[it + 1]
        scatter(2, mine)
        trade = remote(mine, part_in.at[it], core_send.at[it + 2], core_recv.at[it + 2], sibling, x)
        trade.start()
        trade.wait()
        for f in range(2):
            total = part[it + 1, f * PICKS : (f + 1) * PICKS, :] + part_in[it, f * PICKS : (f + 1) * PICKS, :]
            rows = slice(f * CHIPS, f * CHIPS + PICKS)
            table[rows, :] = jnp.maximum(table[rows, :] - total * scale[...], 0.0)
        return carry

    lax.fori_loop(0, ITER_C, sweep, 0)

    for g in range(CHIPS // 8):
        for f in range(2):
            back[pl.ds(32 * g + f, 8, stride=4), :] = gathered(f, g)
    s_buf[...] = jnp.transpose(table[...])
    back[pl.ds(2, CHIPS, stride=4), :] = s_buf[pl.ds(pl.multiple_of(c * CHIPS, CHIPS), CHIPS), :]
    back[pl.ds(3, CHIPS, stride=4), :] = jnp.zeros((CHIPS, K), F32)

    def give(i, carry):
        p = lax.rem(q + i, CHIPS)
        remote(
            back.at[pl.ds(pl.multiple_of(p * 4, 4), 4)],
            back_in.at[pl.ds(pl.multiple_of(q * 4, 4), 4)],
            back_send, back_recv, p * 2 + c, x,
        ).start()
        return carry

    lax.fori_loop(1, CHIPS, give, 0)
    mine = pl.ds(pl.multiple_of(q * 4, 4), 4)
    own_back = pltpu.make_async_copy(back.at[mine], back_in.at[mine], here_sem.at[1])
    own_back.start()
    own_back.wait()
    drain(back_in.at[pl.ds(0, (CHIPS - 1) * 4)], back_recv)

    slot_traces = jnp.concatenate([back_in[pl.ds(0, CHIPS, stride=4), :], back_in[pl.ds(1, CHIPS, stride=4), :]], axis=0)
    hi, lo = split(slot_traces)
    s_all[x, :, 0:K] = hi
    s_all[x, :, K : 2 * K] = lo
    sends = []
    for i in range(1, XS):
        sends.append(remote(s_all.at[x], s_all.at[x], x_send.at[i], x_recv.at[i], me, lax.rem(x + i, XS)))
    for s in sends:
        s.start()

    held = back_in[pl.ds(2, CHIPS, stride=4), :]
    both = jnp.transpose(jnp.concatenate([held, pltpu.roll(held, CHIPS, 1)], axis=0))
    out_traces[0:PICKS, :] = both[0:PICKS]
    out_traces[PICKS:, :] = jnp.maximum(traces[PICKS:, :], 0.0)

    y_own.wait()
    for i in range(1, XS):
        remote(rec, y_all.at[x], y_send.at[i], y_recv.at[i], me, lax.rem(x + i, XS)).wait()
    for s in sends:
        s.wait()

    p_hi = jnp.zeros((K, K), F32)
    p_mix = jnp.zeros((K, K), F32)
    for i in range(XS):
        m = dot_t(s_all[i, :, 0:K], s_all[i])
        p_hi = p_hi + m[:, 0:K]
        p_mix = p_mix + m[:, K : 2 * K]
    p = p_hi + (p_mix + jnp.transpose(p_mix))
    step_row = 1.0 / (1.0 + jnp.sum(jnp.abs(p), axis=0, keepdims=True))
    w_hi, w_lo = split(p * step_row)
    w_buf[0:K, 0:K] = w_hi
    w_buf[0:K, K : 2 * K] = w_lo
    w_buf[K : 2 * K, 0:K] = w_hi
    w_buf[K : 2 * K, K : 2 * K] = jnp.zeros((K, K), BF16)
    for n in range(V // K):
        rows = slice(n * K, (n + 1) * K)
        total = dot(y_all[0, rows, :], s_all[0, :, 0:K])
        for i in range(1, XS):
            total = total + dot(y_all[i, rows, :], s_all[i, :, 0:K])
        start = foot[rows, :].astype(F32)
        q_buf[rows, :] = jnp.where(start > 0.0, total * step_row, -jnp.inf)
        x_buf[rows, :] = start

    def refine(n, carry):
        for k in range(V // K):
            rows = slice(k * K, (k + 1) * K)
            cur = x_buf[rows, :]
            hi, lo = split(cur)
            m = dot(jnp.concatenate([hi, lo], axis=1), w_buf[...])
            moved = cur - (m[:, 0:K] + m[:, K : 2 * K]) + q_buf[rows, :]
            x_buf[rows, :] = jnp.maximum(moved, 0.0)
        return carry

    lax.fori_loop(0, ITER_A, refine, 0)
    out_foot[...] = x_buf[...].astype(BF16)

    drain(grams.at[pl.ds(0, CHIPS - 1)], gram_send)
    drain(msg.at[pl.ds(0, (CHIPS - 1) * 8)], msg_send)
    drain(back.at[pl.ds(0, (CHIPS - 1) * 4)], back_send)


def body(recording, footprints, slot_owner, slot_pick, traces):
    vmem = pl.BlockSpec(memory_space=pltpu.VMEM)
    dma = pltpu.SemaphoreType.DMA
    return pl.pallas_call(
        kernel,
        out_shape=(
            jax.ShapeDtypeStruct(traces.shape, F32),
            jax.ShapeDtypeStruct(footprints.shape, BF16),
        ),
        in_specs=[vmem] * 5,
        out_specs=(vmem, vmem),
        scratch_shapes=[
            pltpu.VMEM((CHIPS, K, K), BF16),
            pltpu.VMEM((CHIPS * 8, K), F32),
            pltpu.VMEM((CHIPS * 8, K), F32),
            pltpu.VMEM((2, CHIPS, K), F32),
            pltpu.VMEM((ITER_C + 1, 2 * PICKS, K), F32),
            pltpu.VMEM((ITER_C, 2 * PICKS, K), F32),
            pltpu.VMEM((PICKS, K), F32),
            pltpu.VMEM((K, K), F32),
            pltpu.VMEM((PICKS, K), F32),
            pltpu.VMEM((K, K), F32),
            pltpu.VMEM((CHIPS * 4, K), F32),
            pltpu.VMEM((CHIPS * 4, K), F32),
            pltpu.VMEM((XS, K, 2 * K), BF16),
            pltpu.VMEM((XS, V, K), BF16),
            pltpu.VMEM((V, K), F32),
            pltpu.VMEM((V, K), F32),
            pltpu.VMEM((8, K), F32),
            pltpu.VMEM((2 * K, 2 * K), BF16),
            pltpu.VMEM((2, CHIPS, K), I32),
            pltpu.VMEM((2, CHIPS, K), I32),
            pltpu.VMEM((CHIPS, K), I32),
            pltpu.VMEM((CHIPS, K), I32),
            pltpu.VMEM((2, 2, CHIPS, K), F32),
            dma,
            dma((RING,)),
            dma((4, 2, RING)),
            dma,
            dma,
            dma((ITER_C + 2,)),
            dma((ITER_C + 2,)),
            dma,
            dma,
            dma((XS,)),
            dma((XS,)),
            dma((XS,)),
            dma((XS,)),
            dma((2,)),
        ],
        compiler_params=pltpu.CompilerParams(
            collective_id=0, has_side_effects=True, vmem_limit_bytes=40 << 20
        ),
    )(recording, footprints, slot_owner.reshape(1, K), slot_pick.reshape(1, K), traces)


def solution(mesh):
    in_specs = (P("tile", "frame"), P("tile", None), P("tile", None), P("tile"), P("tile", "frame"))
    out_specs = (P("tile", "frame"), P("tile", None))
    return jax.shard_map(body, mesh=mesh, in_specs=in_specs, out_specs=out_specs, check_vma=False)
```

time: 249 us -> 74.5 us (0.30)
  blocking collectives: 135 us -> 0 us
  Pallas kernels: 0 us -> 68.3 us
  waiting for transfers between devices: 47 us -> 0 us
  starting transfers between devices: 37.2 us -> 0 us
  matrix products: 10.6 us -> 0 us
  local copies, waits for them, and re-layouts: 14.2 us -> 4.84 us
    all_to_all x8 -> x0, blocking collectives: 135 us -> none  [the longest x3 53.4 us: body(): lax.all_to_all(asked, 'tile', split_axis=0, concat_axis=0, tiled=True)]
    pallas_call x0 -> x1, Pallas kernels: none -> 68.3 us  [body(): pl.pallas_call(kernel, out_shape=(jax.ShapeDtypeStruct(traces.shape, F32)...]
    all_to_all x5 -> x0, waiting for transfers between devices: 47 us -> none  [the longest x2 24.1 us: body(): lax.all_to_all(asked, 'tile', split_axis=0, concat_axis=0, tiled=True)]
    all_to_all x5 -> x0, starting transfers between devices: 37.2 us -> none  [the longest x1 18.4 us: in_one_piece(): lax.all_to_all(both, axis, split_axis=split_dim, concat_axis=concat_dim,...]
    dot_general x26 -> x0, matrix products: 10.6 us -> none  [the longest x5 3.32 us: body(): jnp.dot(select, current, precision=lax.Precision.HIGHEST)]
    scatter x7 -> x0, local copies, waits for them, and re-layouts: 6.69 us -> none  [spread_rows(): filled = jnp.zeros((tile_count * capacity,) + values.shape[1:], values.dt...]
    unnamed x11 -> x12, local copies, waits for them, and re-layouts: 1.41 us -> 4.84 us
    gather x5 -> x0, local copies, waits for them, and re-layouts: 3.22 us -> none  [body(): jnp.take(arrived.reshape(buffer_size, frame_count), buffer_row, axis=0)]
  transfers between devices with their start and end apart: 5 -> 0, of which waited for: 5 -> 0; matrix products, arithmetic and copies ran while one was open for 1% -> 0% of each run, Pallas kernels for 0% -> 0%
where the time goes in v2:
time: 74.5 us; the launch traced here: 73.8 us
  Pallas kernels  68.3 us (92%)
  local copies, waits for them, and re-layouts  4.84 us (6%)
    pallas_call x1, Pallas kernels, body(): pl.pallas_call(kernel, out_shape=(jax.ShapeDtypeStruct(traces.shape, F32)...  68.3 us
    unnamed x12, local copies, waits for them, and re-layouts  4.84 us

profile of v2, /device:TPU:1, one launch (start us, length us, event | category | flops | bytes accessed | tf_op | source)
XLA Modules:
  0.0 73.8 jit_solution(5411676611017971886)
XLA Ops:
  0.6 0.0 copy-start.3
  0.6 0.0 copy-start.4
  0.7 0.6 copy-done.3
  1.3 0.0 copy-done.4
  1.3 0.0 copy-start
  1.3 0.9 %copy-done = bf16[1024,128]{1,0:T(8,128)(2,1)S(1)} copy-done((bf16[1024,128]{1,0:T(8,128)(2,1)S(1)}, bf16[1024,128]{1,0:T(8,128)(2,1)}, u32[]{:S(2)}) %copy-start) | copy-done | bytes 262168
  2.3 0.0 copy-start.1
  2.3 0.9 %copy-done.1 = bf16[1024,128]{1,0:T(8,128)(2,1)S(1)} copy-done((bf16[1024,128]{1,0:T(8,128)(2,1)S(1)}, bf16[1024,128]{1,0:T(8,128)(2,1)}, u32[]{:S(2)}) %copy-start.1) | copy-done | bytes 262168
  3.2 0.0 copy-start.2
  3.2 0.9 %copy-done.2 = f32[320,128]{1,0:T(8,128)S(1)} copy-done((f32[320,128]{1,0:T(8,128)S(1)}, f32[320,128]{1,0:T(8,128)}, u32[]{:S(2)}) %copy-start.2) | copy-done | bytes 163864
  4.1 68.3 %shard_map.68 = (f32[320,128]{1,0:T(8,128)S(1)}, bf16[1024,128]{1,0:T(8,128)(2,1)S(1)}) custom-call(bf16[1024,128]{1,0:T(8,128)(2,1)S(1)} %copy-done, bf16[1024,128]{1,0:T(8,128)(2,1)S(1)} %copy-done.1, s32[1,128]{1,0:T(1,128)S(1)} %bitcast.2, s32[1,128]{1,0:T(1,128)S(1)} %bitcast.3, f32[320,128]{1,0:T(8,128)S(1)} %copy-done.2), custom_call_target="tpu_custom_call" | custom-call | tf_op jit(solution)/shard_map/pallas_call | solution.py:377
  72.5 0.7 copy.9
  73.1 0.7 copy.10
Async XLA Ops:
  0.6 0.7 copy-start.3
  0.6 0.7 copy-start.4
  1.3 0.9 %copy-start = (bf16[1024,128]{1,0:T(8,128)(2,1)S(1)}, bf16[1024,128]{1,0:T(8,128)(2,1)}, u32[]{:S(2)}) copy-start(bf16[1024,128]{1,0:T(8,128)(2,1)} %rec.1) | copy-start | bytes 786436
  2.3 0.9 %copy-start.1 = (bf16[1024,128]{1,0:T(8,128)(2,1)S(1)}, bf16[1024,128]{1,0:T(8,128)(2,1)}, u32[]{:S(2)}) copy-start(bf16[1024,128]{1,0:T(8,128)(2,1)} %foot.1) | copy-start | bytes 786436
  3.2 0.9 %copy-start.2 = (f32[320,128]{1,0:T(8,128)S(1)}, f32[320,128]{1,0:T(8,128)}, u32[]{:S(2)}) copy-start(f32[320,128]{1,0:T(8,128)} %traces.1) | copy-start | bytes 491524

commit v3 on v2

--- a/solution.py
+++ b/solution.py
@@ -7,6 +7,8 @@
 
 ITER_C = 4
 ITER_A = 8
+LATE = 8
+TELL = 7
 RING = 8
 CHIPS = 64
 XS = 4
@@ -57,11 +59,12 @@
 
 
 def kernel(
+    rec_hbm, foot_hbm, owner_hbm, pick_hbm, traces_hbm,
+    out_traces, out_foot,
     rec, foot, owner_in, pick_in, traces,
-    out_traces, out_foot,
-    grams, msg, got, half, part, part_in, bound_in, table, scale, s_buf, back, back_in, s_all, y_all, x_buf, q_buf, a_buf, w_buf,
+    grams, msg, got, half, part, part_in, bound_in, table, scale, s_buf, back, back_in, s_all, y_all, x_buf, q_buf, w_buf,
     pick_s, slot_s, lane_s, rank_s, turn,
-    gram_send, gram_one, gram_two, msg_send, msg_recv, core_send, core_recv, back_send, back_recv, x_send, x_recv, y_send, y_recv, here_sem,
+    gram_send, gram_one, gram_two, msg_send, msg_recv, core_send, core_recv, back_send, back_recv, x_send, x_recv, y_send, y_recv, here_sem, load_sem, ready,
 ):
     me = lax.axis_index("tile")
     x = lax.axis_index("frame")
@@ -73,16 +76,29 @@
     b = yc * (1 - c) + zc * c
     sa, sb = RING - (RING - 1) * c, 1 + (RING - 1) * c
 
+    def ring_a(r):
+        return (lax.rem(a + r, RING) * sa + b * sb) * 2 + c
+
+    def ring_b(r):
+        return (a * sa + lax.rem(b + r, RING) * sb) * 2 + c
+
+    loads = [
+        pltpu.make_async_copy(src, dst, load_sem.at[n])
+        for n, (src, dst) in enumerate(
+            ((foot_hbm, foot), (rec_hbm, rec), (owner_hbm, owner_in), (pick_hbm, pick_in), (traces_hbm, traces))
+        )
+    ]
+    for load in loads:
+        load.start()
     barrier = pltpu.get_barrier_semaphore()
-
-    def greet(i, carry):
-        pl.semaphore_signal(barrier, inc=1, device_id=(lax.rem(q + i, CHIPS) * 2 + c, x), device_id_type=MESH)
-        return carry
-
-    lax.fori_loop(1, CHIPS, greet, 0)
-    pl.semaphore_signal(barrier, inc=1, device_id=(sibling, x), device_id_type=MESH)
+    for r in (4, 3, 5, 2, 6, 1, 7):
+        pl.semaphore_signal(barrier, inc=1, device_id=(ring_a(r), x), device_id_type=MESH)
+        pl.semaphore_signal(barrier, inc=1, device_id=(ring_b(r), x), device_id_type=MESH)
     for i in range(1, XS):
         pl.semaphore_signal(barrier, inc=1, device_id=(me, lax.rem(x + i, XS)), device_id_type=MESH)
+    pl.semaphore_signal(barrier, inc=1, device_id=(sibling, x), device_id_type=MESH)
+    for load in loads:
+        load.wait()
 
     block = foot[...]
     gram = dot_t(block, block)
@@ -91,6 +107,7 @@
     bound = jnp.sum(jnp.abs(gram), axis=0, keepdims=True)
     lane = lax.broadcasted_iota(I32, (K, K), 1)
     sub = lax.broadcasted_iota(I32, (K, K), 0)
+    rest = jnp.sum(jnp.where(lane == sub, gram - gram.astype(BF16).astype(F32), 0.0), axis=0, keepdims=True)
     own = owner_in[...]
     own = jnp.broadcast_to((own & 1) * CHIPS + (own >> 1), (K, K))
     own_t = jnp.transpose(own.astype(F32)).astype(I32)
@@ -113,86 +130,93 @@
         jnp.broadcast_to(code1, (CHIPS, K)),
         jnp.broadcast_to(slot_code, (CHIPS, K)),
         jnp.broadcast_to(bound, (CHIPS, K)),
-        jnp.zeros((CHIPS, K), F32),
+        jnp.broadcast_to(rest, (CHIPS, K)),
     )
     for j, row in enumerate(rows):
         msg[pl.ds(j, CHIPS, stride=8), :] = row
     got[pl.ds(pl.multiple_of(q * 8, 8), 8), :] = msg[pl.ds(pl.multiple_of(q * 8, 8), 8), :]
 
-    pl.semaphore_wait(barrier, CHIPS - 1 + 1 + XS - 1)
-
-    up = (a * sa + lax.rem(b + 1, RING) * sb) * 2 + c
-    down = (a * sa + lax.rem(b + RING - 1, RING) * sb) * 2 + c
-
-    def forward(step, i, off, want_up, want_down):
-        r = ring_order(i)
-        column = lax.rem(a + r, RING) * sa
-        if want_up:
+    pl.semaphore_wait(barrier, 2 * (RING - 1) + XS)
+    for r in (4, 3, 5, 2, 6, 1, 7):
+        pl.semaphore_signal(ready, inc=1, device_id=(ring_b(r), x), device_id_type=MESH)
+
+    def forward(i, off, hop, up=True, down=True):
+        column = lax.rem(a + ring_order(i), RING) * sa
+        if up:
             p = column + lax.rem(b + RING - off, RING) * sb
-            remote(grams.at[p], grams.at[p], gram_send, gram_two.at[step, 0, i], up, x).start()
-        if want_down:
+            remote(grams.at[p], grams.at[p], gram_send, gram_two.at[off + hop - 1, 0, i], ring_b(hop), x).start()
+        if down:
             p = column + lax.rem(b + off, RING) * sb
-            remote(grams.at[p], grams.at[p], gram_send, gram_two.at[step, 1, i], down, x).start()
-
-    forward(0, 0, 0, True, True)
-
-    def first(i, carry):
-        r = ring_order(i)
-        peer = (lax.rem(a + RING - r, RING) * sa + b * sb) * 2 + c
-        remote(grams.at[q], grams.at[q], gram_send, gram_one.at[i], peer, x).start()
-        return carry
-
-    lax.fori_loop(1, RING, first, 0)
-
-    def tell(i, carry):
-        p = lax.rem(q + i, CHIPS)
+            remote(grams.at[p], grams.at[p], gram_send, gram_two.at[off + hop - 1, 1, i], ring_b(RING - hop), x).start()
+
+    def arrived(off, i, up=True, down=True):
+        if up:
+            pltpu.make_async_copy(grams.at[0], grams.at[0], gram_two.at[off - 1, 0, i]).wait()
+        if down:
+            pltpu.make_async_copy(grams.at[0], grams.at[0], gram_two.at[off - 1, 1, i]).wait()
+
+    def tell(n):
+        rz, ry = ring_order(RING - 1 - n // RING), ring_order(RING - 1 - lax.rem(n, RING))
+        p = lax.rem(zc + rz, RING) * RING + lax.rem(yc + ry, RING)
         remote(
             msg.at[pl.ds(pl.multiple_of(p * 8, 8), 8)],
             got.at[pl.ds(pl.multiple_of(q * 8, 8), 8)],
             msg_send, msg_recv, p * 2 + c, x,
         ).start()
-        return carry
-
-    lax.fori_loop(1, CHIPS, tell, 0)
+
+    def loop(start, stop, step):
+        def run(i, carry):
+            step(i)
+            return carry
+
+        lax.fori_loop(start, stop, run, 0)
+
+    forward(0, 0, 1)
+    loop(1, RING, lambda i: remote(
+        grams.at[q], grams.at[q], gram_send, gram_one.at[RING - i], ring_a(RING - ring_order(RING - i)), x
+    ).start())
     for i in range(1, XS):
         remote(rec, y_all.at[x], y_send.at[i], y_recv.at[i], me, lax.rem(x + i, XS)).start()
     y_own = pltpu.make_async_copy(rec, y_all.at[x], here_sem.at[0])
     y_own.start()
 
-    def pass_on(i, carry):
+    def pass_on(i):
         pltpu.make_async_copy(grams.at[0], grams.at[0], gram_one.at[i]).wait()
-        forward(0, i, 0, True, True)
-        return carry
-
-    lax.fori_loop(1, RING, pass_on, 0)
-
-    def arrived(step, side, i):
-        pltpu.make_async_copy(grams.at[0], grams.at[0], gram_two.at[step, side, i]).wait()
-
-    for step in range(1, 3):
-
-        def hop(i, carry, step=step):
-            arrived(step - 1, 0, i)
-            arrived(step - 1, 1, i)
-            forward(step, i, step, True, True)
-            return carry
-
-        lax.fori_loop(0, RING, hop, 0)
-
-    def last_up(i, carry):
-        arrived(2, 0, i)
-        arrived(2, 1, i)
-        forward(3, i, 3, True, False)
-        return carry
-
-    def last_down(i, carry):
-        arrived(2, 0, i)
-        arrived(2, 1, i)
-        forward(3, i, 3, False, True)
-        return carry
-
-    lax.fori_loop(0, RING // 2, last_up, 0)
-    lax.fori_loop(RING // 2, RING, last_down, 0)
+        forward(i, 0, 1)
+
+    def some(n):
+        loop(n * TELL, (n + 1) * TELL, tell)
+
+    loop(1, LATE, pass_on)
+    pl.semaphore_wait(ready, RING - 1)
+
+    def pass_late(i):
+        pass_on(i)
+        forward(i, 0, 2)
+        some(i - LATE)
+
+    loop(LATE, RING, pass_late)
+
+    def second(i):
+        arrived(1, i)
+        forward(i, 1, 1)
+        some(RING - LATE + i)
+
+    loop(0, LATE, second)
+    loop(RING * TELL, CHIPS - 1, tell)
+
+    def third_up(i):
+        arrived(2, i)
+        forward(i, 2, 1)
+        forward(i, 2, 2, down=False)
+
+    def third_down(i):
+        arrived(2, i)
+        forward(i, 2, 1)
+        forward(i, 2, 2, up=False)
+
+    loop(0, RING // 2, third_up)
+    loop(RING // 2, RING, third_down)
 
     drain(got.at[pl.ds(0, (CHIPS - 1) * 8)], msg_recv)
     half[c] = got[pl.ds(2, CHIPS, stride=8), :]
@@ -247,25 +271,23 @@
         second_rank = jnp.take_along_axis(pick_rows(table, f * CHIPS, pick_s[1, s8, :]), lanes, axis=1)
         return jnp.where(rank_s[s8, :] == 0, first_rank, second_rank)
 
-    for i in range(4):
-        def last(k, carry, i=i):
-            arrived(3, i // 2, k)
-            return carry
-        if i == 0:
-            lax.fori_loop(0, RING // 2, last, 0)
-        if i == 2:
-            lax.fori_loop(RING // 2, RING, last, 0)
+    loop(LATE, RING, lambda i: arrived(1, i))
+    loop(0, RING, lambda i: arrived(3, i))
+    loop(0, RING // 2, lambda i: arrived(4, i, down=False))
+    loop(RING // 2, RING, lambda i: arrived(4, i, up=False))
 
     sub8 = lax.broadcasted_iota(I32, (8, K), 0)
 
     def sweep(it, carry):
         for g in range(CHIPS // 8):
             s8 = slice(8 * g, 8 * g + 8)
-            h0, l0 = split(gathered(0, g))
-            h1, l1 = split(gathered(1, g))
+            s0, s1 = gathered(0, g), gathered(1, g)
+            h0, l0 = split(s0)
+            h1, l1 = split(s1)
+            extra = got[pl.ds(64 * g + 7, 8, stride=8), :]
             left = jnp.concatenate([h0, l0, h1, l1], axis=0)
-            g0 = -got[pl.ds(64 * g, 8, stride=8), :]
-            g1 = -got[pl.ds(64 * g + 1, 8, stride=8), :]
+            g0 = extra * s0 - got[pl.ds(64 * g, 8, stride=8), :]
+            g1 = extra * s1 - got[pl.ds(64 * g + 1, 8, stride=8), :]
             for j in range(8):
                 m = dot(left, grams[8 * g + j])
                 g0 = g0 + jnp.where(sub8 == j, m[0:8] + m[8:16], 0.0)
@@ -294,16 +316,14 @@
     back[pl.ds(2, CHIPS, stride=4), :] = s_buf[pl.ds(pl.multiple_of(c * CHIPS, CHIPS), CHIPS), :]
     back[pl.ds(3, CHIPS, stride=4), :] = jnp.zeros((CHIPS, K), F32)
 
-    def give(i, carry):
-        p = lax.rem(q + i, CHIPS)
+    away = [(rz, ry) for rz in range(RING) for ry in range(RING) if rz or ry]
+    for rz, ry in sorted(away, key=lambda r: -min(r[0], RING - r[0]) - min(r[1], RING - r[1])):
+        p = lax.rem(zc + rz, RING) * RING + lax.rem(yc + ry, RING)
         remote(
             back.at[pl.ds(pl.multiple_of(p * 4, 4), 4)],
             back_in.at[pl.ds(pl.multiple_of(q * 4, 4), 4)],
             back_send, back_recv, p * 2 + c, x,
         ).start()
-        return carry
-
-    lax.fori_loop(1, CHIPS, give, 0)
     mine = pl.ds(pl.multiple_of(q * 4, 4), 4)
     own_back = pltpu.make_async_copy(back.at[mine], back_in.at[mine], here_sem.at[1])
     own_back.start()
@@ -380,9 +400,14 @@
             jax.ShapeDtypeStruct(traces.shape, F32),
             jax.ShapeDtypeStruct(footprints.shape, BF16),
         ),
-        in_specs=[vmem] * 5,
+        in_specs=[pl.BlockSpec(memory_space=pltpu.HBM)] * 5,
         out_specs=(vmem, vmem),
         scratch_shapes=[
+            pltpu.VMEM((V, K), BF16),
+            pltpu.VMEM((V, K), BF16),
+            pltpu.VMEM((1, K), I32),
+            pltpu.VMEM((1, K), I32),
+            pltpu.VMEM(traces.shape, F32),
             pltpu.VMEM((CHIPS, K, K), BF16),
             pltpu.VMEM((CHIPS * 8, K), F32),
             pltpu.VMEM((CHIPS * 8, K), F32),
@@ -399,7 +424,6 @@
             pltpu.VMEM((XS, V, K), BF16),
             pltpu.VMEM((V, K), F32),
             pltpu.VMEM((V, K), F32),
-            pltpu.VMEM((8, K), F32),
             pltpu.VMEM((2 * K, 2 * K), BF16),
             pltpu.VMEM((2, CHIPS, K), I32),
             pltpu.VMEM((2, CHIPS, K), I32),
@@ -420,6 +444,8 @@
             dma((XS,)),
             dma((XS,)),
             dma((2,)),
+            dma((5,)),
+            pltpu.SemaphoreType.REGULAR,
         ],
         compiler_params=pltpu.CompilerParams(
             collective_id=0, has_side_effects=True, vmem_limit_bytes=40 << 20

time: 74.5 us -> 70.5 us (0.946)
  Pallas kernels: 68.3 us -> 64.8 us
    pallas_call x1, Pallas kernels: 68.3 us -> 64.8 us  [body(): pl.pallas_call(kernel, out_shape=(jax.ShapeDtypeStruct(traces.shape, F32)...]
where the time goes in v3:
time: 70.5 us; the launch traced here: 70.3 us
  Pallas kernels  64.8 us (92%)
  local copies, waits for them, and re-layouts  4.84 us (7%)
    pallas_call x1, Pallas kernels, body(): pl.pallas_call(kernel, out_shape=(jax.ShapeDtypeStruct(traces.shape, F32)...  64.8 us
    unnamed x12, local copies, waits for them, and re-layouts  4.84 us

profile of v3, /device:TPU:1, one launch (start us, length us, event | category | flops | bytes accessed | tf_op | source)
XLA Modules:
  0.0 70.3 jit_solution(11751246709854982916)
XLA Ops:
  0.6 0.0 copy-start.3
  0.6 0.0 copy-start.4
  0.7 0.6 copy-done.3
  1.3 0.0 copy-done.4
  1.3 0.0 copy-start
  1.3 0.9 %copy-done = bf16[1024,128]{1,0:T(8,128)(2,1)S(1)} copy-done((bf16[1024,128]{1,0:T(8,128)(2,1)S(1)}, bf16[1024,128]{1,0:T(8,128)(2,1)}, u32[]{:S(2)}) %copy-start) | copy-done | bytes 262168
  2.3 0.0 copy-start.1
  2.3 0.9 %copy-done.1 = bf16[1024,128]{1,0:T(8,128)(2,1)S(1)} copy-done((bf16[1024,128]{1,0:T(8,128)(2,1)S(1)}, bf16[1024,128]{1,0:T(8,128)(2,1)}, u32[]{:S(2)}) %copy-start.1) | copy-done | bytes 262168
  3.2 0.0 copy-start.2
  3.2 0.9 %copy-done.2 = f32[320,128]{1,0:T(8,128)S(1)} copy-done((f32[320,128]{1,0:T(8,128)S(1)}, f32[320,128]{1,0:T(8,128)}, u32[]{:S(2)}) %copy-start.2) | copy-done | bytes 163864
  4.1 64.8 %shard_map.68 = (f32[320,128]{1,0:T(8,128)S(1)}, bf16[1024,128]{1,0:T(8,128)(2,1)S(1)}) custom-call(bf16[1024,128]{1,0:T(8,128)(2,1)S(1)} %copy-done, bf16[1024,128]{1,0:T(8,128)(2,1)S(1)} %copy-done.1, s32[1,128]{1,0:T(1,128)S(1)} %bitcast.2, s32[1,128]{1,0:T(1,128)S(1)} %bitcast.3, f32[320,128]{1,0:T(8,128)S(1)} %copy-done.2), custom_call_target="tpu_custom_call" | custom-call | tf_op jit(solution)/shard_map/pallas_call | solution.py:397
  69.0 0.7 copy.9
  69.6 0.7 copy.10
Async XLA Ops:
  0.6 0.7 copy-start.3
  0.6 0.7 copy-start.4
  1.3 0.9 %copy-start = (bf16[1024,128]{1,0:T(8,128)(2,1)S(1)}, bf16[1024,128]{1,0:T(8,128)(2,1)}, u32[]{:S(2)}) copy-start(bf16[1024,128]{1,0:T(8,128)(2,1)} %rec_hbm.1) | copy-start | bytes 786436
  2.3 0.9 %copy-start.1 = (bf16[1024,128]{1,0:T(8,128)(2,1)S(1)}, bf16[1024,128]{1,0:T(8,128)(2,1)}, u32[]{:S(2)}) copy-start(bf16[1024,128]{1,0:T(8,128)(2,1)} %foot_hbm.1) | copy-start | bytes 786436
  3.2 0.9 %copy-start.2 = (f32[320,128]{1,0:T(8,128)S(1)}, f32[320,128]{1,0:T(8,128)}, u32[]{:S(2)}) copy-start(f32[320,128]{1,0:T(8,128)} %traces_hbm.1) | copy-start | bytes 491524

commit v4 on v3

--- a/solution.py
+++ b/solution.py
@@ -9,6 +9,8 @@
 ITER_A = 8
 LATE = 8
 TELL = 7
+SENT = 7
+ROWS = 256
 RING = 8
 CHIPS = 64
 XS = 4
@@ -62,7 +64,7 @@
     rec_hbm, foot_hbm, owner_hbm, pick_hbm, traces_hbm,
     out_traces, out_foot,
     rec, foot, owner_in, pick_in, traces,
-    grams, msg, got, half, part, part_in, bound_in, table, scale, s_buf, back, back_in, s_all, y_all, x_buf, q_buf, w_buf,
+    grams, packed, msg, got, half, part, part_in, bound_in, table, scale, s_buf, back, back_in, s_all, y_all, x_buf, q_buf, w_buf,
     pick_s, slot_s, lane_s, rank_s, turn,
     gram_send, gram_one, gram_two, msg_send, msg_recv, core_send, core_recv, back_send, back_recv, x_send, x_recv, y_send, y_recv, here_sem, load_sem, ready,
 ):
@@ -104,6 +106,10 @@
     gram = dot_t(block, block)
     drive = dot_t(rec[...], block)
     grams[q] = gram.astype(BF16)
+    right = lax.broadcasted_iota(I32, (K // 4, K), 1) >= K // 2
+    fold = jnp.where(right, gram[K // 2 : 3 * K // 4], pltpu.roll(gram[3 * K // 4 :], K // 2, 1))
+    packed[q, 0 : K // 2] = gram[0 : K // 2].astype(BF16)
+    packed[q, K // 2 :] = fold.astype(BF16)
     bound = jnp.sum(jnp.abs(gram), axis=0, keepdims=True)
     lane = lax.broadcasted_iota(I32, (K, K), 1)
     sub = lax.broadcasted_iota(I32, (K, K), 0)
@@ -111,30 +117,26 @@
     own = owner_in[...]
     own = jnp.broadcast_to((own & 1) * CHIPS + (own >> 1), (K, K))
     own_t = jnp.transpose(own.astype(F32)).astype(I32)
-    pick_t = jnp.transpose(jnp.broadcast_to(pick_in[...], (K, K)).astype(F32)).astype(I32)
     same = own == own_t
-    rank_row = jnp.sum(jnp.where(same & (sub < lane), 1.0, 0.0), axis=0, keepdims=True)
     rank_col = jnp.sum(jnp.where(same & (lane < sub), 1.0, 0.0), axis=1, keepdims=True)
-    code = (pick_t * K + sub + 1).astype(F32)
-    here = own_t == lane
-    code0 = jnp.sum(jnp.where(here & (rank_col < 0.5), code, 0.0), axis=0, keepdims=True)
-    code1 = jnp.sum(jnp.where(here & (rank_col > 0.5), code, 0.0), axis=0, keepdims=True)
-    slot_code = own[0:1, :].astype(F32) * 2.0 + rank_row
+    place = (sub + 1).astype(F32) * jnp.where(rank_col < 0.5, 1.0, 2.0 * K)
+    slots_of = jnp.sum(jnp.where(own_t == lane, place, 0.0), axis=0, keepdims=True)
+    slot_row = (own[0:1, :] * CHIPS + pick_in[...]).astype(F32)
     by_frame = jnp.transpose(traces[0:K, :])
     low_lane = lax.broadcasted_iota(I32, (CHIPS, K), 1) < CHIPS
     rows = (
         drive[0:CHIPS],
         drive[CHIPS:K],
         jnp.where(low_lane, by_frame[0:CHIPS], pltpu.roll(by_frame[CHIPS:K], CHIPS, 1)),
-        jnp.broadcast_to(code0, (CHIPS, K)),
-        jnp.broadcast_to(code1, (CHIPS, K)),
-        jnp.broadcast_to(slot_code, (CHIPS, K)),
+        jnp.broadcast_to(slots_of, (CHIPS, K)),
+        jnp.broadcast_to(slot_row, (CHIPS, K)),
         jnp.broadcast_to(bound, (CHIPS, K)),
         jnp.broadcast_to(rest, (CHIPS, K)),
     )
     for j, row in enumerate(rows):
         msg[pl.ds(j, CHIPS, stride=8), :] = row
-    got[pl.ds(pl.multiple_of(q * 8, 8), 8), :] = msg[pl.ds(pl.multiple_of(q * 8, 8), 8), :]
+    for j, row in enumerate(rows):
+        got[pl.ds(q * 8 + j, 1), :] = msg[pl.ds(q * 8 + j, 1), :]
 
     pl.semaphore_wait(barrier, 2 * (RING - 1) + XS)
     for r in (4, 3, 5, 2, 6, 1, 7):
@@ -144,23 +146,38 @@
         column = lax.rem(a + ring_order(i), RING) * sa
         if up:
             p = column + lax.rem(b + RING - off, RING) * sb
-            remote(grams.at[p], grams.at[p], gram_send, gram_two.at[off + hop - 1, 0, i], ring_b(hop), x).start()
+            remote(packed.at[p], packed.at[p], gram_send, gram_two.at[off + hop - 1, 0, i], ring_b(hop), x).start()
         if down:
             p = column + lax.rem(b + off, RING) * sb
-            remote(grams.at[p], grams.at[p], gram_send, gram_two.at[off + hop - 1, 1, i], ring_b(RING - hop), x).start()
+            remote(packed.at[p], packed.at[p], gram_send, gram_two.at[off + hop - 1, 1, i], ring_b(RING - hop), x).start()
+
+    def unfold(p):
+        high = packed[p, 0 : K // 2]
+        fold = packed[p, K // 2 :]
+        grams[p, 0 : K // 2] = high
+        grams[p, K // 2 : 3 * K // 4] = fold
+        grams[p, 3 * K // 4 :] = pltpu.roll(fold.astype(F32), K // 2, 1).astype(BF16)
+        grams[p, K // 2 :, 0 : K // 2] = jnp.transpose(high.astype(F32))[K // 2 :].astype(BF16)
+
+    def unfolded(i, off, up=True, down=True):
+        column = lax.rem(a + ring_order(i), RING) * sa
+        if up:
+            unfold(column + lax.rem(b + RING - off, RING) * sb)
+        if down:
+            unfold(column + lax.rem(b + off, RING) * sb)
 
     def arrived(off, i, up=True, down=True):
         if up:
-            pltpu.make_async_copy(grams.at[0], grams.at[0], gram_two.at[off - 1, 0, i]).wait()
+            pltpu.make_async_copy(packed.at[0], packed.at[0], gram_two.at[off - 1, 0, i]).wait()
         if down:
-            pltpu.make_async_copy(grams.at[0], grams.at[0], gram_two.at[off - 1, 1, i]).wait()
+            pltpu.make_async_copy(packed.at[0], packed.at[0], gram_two.at[off - 1, 1, i]).wait()
 
     def tell(n):
         rz, ry = ring_order(RING - 1 - n // RING), ring_order(RING - 1 - lax.rem(n, RING))
         p = lax.rem(zc + rz, RING) * RING + lax.rem(yc + ry, RING)
         remote(
-            msg.at[pl.ds(pl.multiple_of(p * 8, 8), 8)],
-            got.at[pl.ds(pl.multiple_of(q * 8, 8), 8)],
+            msg.at[pl.ds(pl.multiple_of(p * 8, 8), SENT)],
+            got.at[pl.ds(pl.multiple_of(q * 8, 8), SENT)],
             msg_send, msg_recv, p * 2 + c, x,
         ).start()
 
@@ -173,7 +190,7 @@
 
     forward(0, 0, 1)
     loop(1, RING, lambda i: remote(
-        grams.at[q], grams.at[q], gram_send, gram_one.at[RING - i], ring_a(RING - ring_order(RING - i)), x
+        packed.at[q], packed.at[q], gram_send, gram_one.at[RING - i], ring_a(RING - ring_order(RING - i)), x
     ).start())
     for i in range(1, XS):
         remote(rec, y_all.at[x], y_send.at[i], y_recv.at[i], me, lax.rem(x + i, XS)).start()
@@ -181,8 +198,9 @@
     y_own.start()
 
     def pass_on(i):
-        pltpu.make_async_copy(grams.at[0], grams.at[0], gram_one.at[i]).wait()
+        pltpu.make_async_copy(packed.at[0], packed.at[0], gram_one.at[i]).wait()
         forward(i, 0, 1)
+        unfolded(i, 0, down=False)
 
     def some(n):
         loop(n * TELL, (n + 1) * TELL, tell)
@@ -201,6 +219,7 @@
         arrived(1, i)
         forward(i, 1, 1)
         some(RING - LATE + i)
+        unfolded(i, 1)
 
     loop(0, LATE, second)
     loop(RING * TELL, CHIPS - 1, tell)
@@ -209,26 +228,34 @@
         arrived(2, i)
         forward(i, 2, 1)
         forward(i, 2, 2, down=False)
+        unfolded(i, 2)
 
     def third_down(i):
         arrived(2, i)
         forward(i, 2, 1)
         forward(i, 2, 2, up=False)
+        unfolded(i, 2)
 
     loop(0, RING // 2, third_up)
     loop(RING // 2, RING, third_down)
 
-    drain(got.at[pl.ds(0, (CHIPS - 1) * 8)], msg_recv)
+    drain(got.at[pl.ds(0, (CHIPS - 1) * SENT)], msg_recv)
     half[c] = got[pl.ds(2, CHIPS, stride=8), :]
     swap = remote(half.at[c], half.at[c], core_send.at[0], core_recv.at[0], sibling, x)
     swap.start()
-    for r in range(2):
-        m = got[pl.ds(3 + r, CHIPS, stride=8), :].astype(I32) - 1
-        pick_s[r] = m >> 7
-        slot_s[r] = m & (K - 1)
-    m = got[pl.ds(5, CHIPS, stride=8), :].astype(I32)
-    lane_s[...] = m >> 1
-    rank_s[...] = m & 1
+    slot_count = lax.broadcasted_iota(I32, (8, K), 1)
+    for g in range(CHIPS // 8):
+        s8 = slice(8 * g, 8 * g + 8)
+        places = got[pl.ds(64 * g + 3, 8, stride=8), :].astype(I32)
+        slots = got[pl.ds(64 * g + 4, 8, stride=8), :].astype(I32)
+        lanes = slots >> 6
+        picks = slots & (CHIPS - 1)
+        for r, place in enumerate(((places & (2 * K - 1)) - 1, (places >> 8) - 1)):
+            slot = place & (K - 1)
+            slot_s[r, s8, :] = slot
+            pick_s[r, s8, :] = jnp.where(place >= 0, jnp.take_along_axis(picks, slot, axis=1), -1)
+        lane_s[s8, :] = lanes
+        rank_s[s8, :] = jnp.where(jnp.take_along_axis(places >> 8, lanes, axis=1) == slot_count + 1, 1, 0)
 
     def scatter(n, into):
         def eight(j, carry):
@@ -251,7 +278,7 @@
 
     for g in range(CHIPS // 8):
         s8 = slice(8 * g, 8 * g + 8)
-        vals = got[pl.ds(64 * g + 6, 8, stride=8), :]
+        vals = got[pl.ds(64 * g + 5, 8, stride=8), :]
         for r in range(2):
             turn[r, 0, s8, :] = jnp.take_along_axis(vals, slot_s[r, s8, :], axis=1)
     scatter(1, part.at[0])
@@ -271,10 +298,17 @@
         second_rank = jnp.take_along_axis(pick_rows(table, f * CHIPS, pick_s[1, s8, :]), lanes, axis=1)
         return jnp.where(rank_s[s8, :] == 0, first_rank, second_rank)
 
-    loop(LATE, RING, lambda i: arrived(1, i))
-    loop(0, RING, lambda i: arrived(3, i))
-    loop(0, RING // 2, lambda i: arrived(4, i, down=False))
-    loop(RING // 2, RING, lambda i: arrived(4, i, up=False))
+    def fetch(off, up, down):
+        def one(i):
+            arrived(off, i, up, down)
+            unfolded(i, off, up, down)
+
+        return one
+
+    loop(LATE, RING, fetch(1, True, True))
+    loop(0, RING, fetch(3, True, True))
+    loop(0, RING // 2, fetch(4, True, False))
+    loop(RING // 2, RING, fetch(4, False, True))
 
     sub8 = lax.broadcasted_iota(I32, (8, K), 0)
 
@@ -284,14 +318,15 @@
             s0, s1 = gathered(0, g), gathered(1, g)
             h0, l0 = split(s0)
             h1, l1 = split(s1)
-            extra = got[pl.ds(64 * g + 7, 8, stride=8), :]
+            extra = got[pl.ds(64 * g + 6, 8, stride=8), :]
             left = jnp.concatenate([h0, l0, h1, l1], axis=0)
             g0 = extra * s0 - got[pl.ds(64 * g, 8, stride=8), :]
             g1 = extra * s1 - got[pl.ds(64 * g + 1, 8, stride=8), :]
-            for j in range(8):
-                m = dot(left, grams[8 * g + j])
-                g0 = g0 + jnp.where(sub8 == j, m[0:8] + m[8:16], 0.0)
-                g1 = g1 + jnp.where(sub8 == j, m[16:24] + m[24:32], 0.0)
+            for j in range(0, 8, 2):
+                m = dot(left, jnp.concatenate([grams[8 * g + j], grams[8 * g + j + 1]], axis=1))
+                f0, f1 = m[0:8] + m[8:16], m[16:24] + m[24:32]
+                g0 = g0 + jnp.where(sub8 == j, f0[:, 0:K], jnp.where(sub8 == j + 1, f0[:, K:], 0.0))
+                g1 = g1 + jnp.where(sub8 == j, f1[:, 0:K], jnp.where(sub8 == j + 1, f1[:, K:], 0.0))
             for r in range(2):
                 slots = slot_s[r, s8, :]
                 turn[r, 0, s8, :] = jnp.take_along_axis(g0, slots, axis=1)
@@ -374,8 +409,8 @@
         x_buf[rows, :] = start
 
     def refine(n, carry):
-        for k in range(V // K):
-            rows = slice(k * K, (k + 1) * K)
+        for k in range(V // ROWS):
+            rows = slice(k * ROWS, (k + 1) * ROWS)
             cur = x_buf[rows, :]
             hi, lo = split(cur)
             m = dot(jnp.concatenate([hi, lo], axis=1), w_buf[...])
@@ -386,8 +421,8 @@
     lax.fori_loop(0, ITER_A, refine, 0)
     out_foot[...] = x_buf[...].astype(BF16)
 
-    drain(grams.at[pl.ds(0, CHIPS - 1)], gram_send)
-    drain(msg.at[pl.ds(0, (CHIPS - 1) * 8)], msg_send)
+    drain(packed.at[pl.ds(0, CHIPS - 1)], gram_send)
+    drain(msg.at[pl.ds(0, (CHIPS - 1) * SENT)], msg_send)
     drain(back.at[pl.ds(0, (CHIPS - 1) * 4)], back_send)
 
 
@@ -409,6 +444,7 @@
             pltpu.VMEM((1, K), I32),
             pltpu.VMEM(traces.shape, F32),
             pltpu.VMEM((CHIPS, K, K), BF16),
+            pltpu.VMEM((CHIPS, 3 * K // 4, K), BF16),
             pltpu.VMEM((CHIPS * 8, K), F32),
             pltpu.VMEM((CHIPS * 8, K), F32),
             pltpu.VMEM((2, CHIPS, K), F32),

time: 70.5 us -> 66.6 us (0.945)
  Pallas kernels: 64.8 us -> 60.8 us
    pallas_call x1, Pallas kernels: 64.8 us -> 60.8 us  [body(): pl.pallas_call(kernel, out_shape=(jax.ShapeDtypeStruct(traces.shape, F32)...]
where the time goes in v4:
time: 66.6 us; the launch traced here: 66.3 us
  Pallas kernels  60.8 us (91%)
  local copies, waits for them, and re-layouts  4.84 us (7%)
    pallas_call x1, Pallas kernels, body(): pl.pallas_call(kernel, out_shape=(jax.ShapeDtypeStruct(traces.shape, F32)...  60.8 us
    unnamed x12, local copies, waits for them, and re-layouts  4.84 us

profile of v4, /device:TPU:1, one launch (start us, length us, event | category | flops | bytes accessed | tf_op | source)
XLA Modules:
  0.0 66.3 jit_solution(16667809450667880761)
XLA Ops:
  0.6 0.0 copy-start.3
  0.6 0.0 copy-start.4
  0.7 0.6 copy-done.3
  1.3 0.0 copy-done.4
  1.3 0.0 copy-start
  1.3 0.9 %copy-done = bf16[1024,128]{1,0:T(8,128)(2,1)S(1)} copy-done((bf16[1024,128]{1,0:T(8,128)(2,1)S(1)}, bf16[1024,128]{1,0:T(8,128)(2,1)}, u32[]{:S(2)}) %copy-start) | copy-done | bytes 262168
  2.3 0.0 copy-start.1
  2.3 0.9 %copy-done.1 = bf16[1024,128]{1,0:T(8,128)(2,1)S(1)} copy-done((bf16[1024,128]{1,0:T(8,128)(2,1)S(1)}, bf16[1024,128]{1,0:T(8,128)(2,1)}, u32[]{:S(2)}) %copy-start.1) | copy-done | bytes 262168
  3.2 0.0 copy-start.2
  3.2 0.9 %copy-done.2 = f32[320,128]{1,0:T(8,128)S(1)} copy-done((f32[320,128]{1,0:T(8,128)S(1)}, f32[320,128]{1,0:T(8,128)}, u32[]{:S(2)}) %copy-start.2) | copy-done | bytes 163864
  4.1 60.8 %shard_map.68 = (f32[320,128]{1,0:T(8,128)S(1)}, bf16[1024,128]{1,0:T(8,128)(2,1)S(1)}) custom-call(bf16[1024,128]{1,0:T(8,128)(2,1)S(1)} %copy-done, bf16[1024,128]{1,0:T(8,128)(2,1)S(1)} %copy-done.1, s32[1,128]{1,0:T(1,128)S(1)} %bitcast.2, s32[1,128]{1,0:T(1,128)S(1)} %bitcast.3, f32[320,128]{1,0:T(8,128)S(1)} %copy-done.2), custom_call_target="tpu_custom_call" | custom-call | tf_op jit(solution)/shard_map/pallas_call | solution.py:432
  64.9 0.7 %copy.9 = f32[320,128]{1,0:T(8,128)} copy(f32[320,128]{1,0:T(8,128)S(1)} %get-tuple-element.4) | data formatting | bytes 327680
  65.5 0.7 %copy.10 = bf16[1024,128]{1,0:T(8,128)(2,1)} copy(bf16[1024,128]{1,0:T(8,128)(2,1)S(1)} %get-tuple-element.5) | data formatting | bytes 524288
Async XLA Ops:
  0.6 0.7 copy-start.3
  0.6 0.7 copy-start.4
  1.3 0.9 %copy-start = (bf16[1024,128]{1,0:T(8,128)(2,1)S(1)}, bf16[1024,128]{1,0:T(8,128)(2,1)}, u32[]{:S(2)}) copy-start(bf16[1024,128]{1,0:T(8,128)(2,1)} %rec_hbm.1) | copy-start | bytes 786436
  2.3 0.9 %copy-start.1 = (bf16[1024,128]{1,0:T(8,128)(2,1)S(1)}, bf16[1024,128]{1,0:T(8,128)(2,1)}, u32[]{:S(2)}) copy-start(bf16[1024,128]{1,0:T(8,128)(2,1)} %foot_hbm.1) | copy-start | bytes 786436
  3.2 0.9 %copy-start.2 = (f32[320,128]{1,0:T(8,128)S(1)}, f32[320,128]{1,0:T(8,128)}, u32[]{:S(2)}) copy-start(f32[320,128]{1,0:T(8,128)} %traces_hbm.1) | copy-start | bytes 491524

commit v5 on v4

--- a/solution.py
+++ b/solution.py
@@ -205,8 +205,14 @@
     def some(n):
         loop(n * TELL, (n + 1) * TELL, tell)
 
-    loop(1, LATE, pass_on)
+    loop(1, 5, pass_on)
     pl.semaphore_wait(ready, RING - 1)
+
+    def pass_and_tell(i):
+        pass_on(i)
+        loop((i - 5) * 9, (i - 5) * 9 + 9, tell)
+
+    loop(5, RING, pass_and_tell)
 
     def pass_late(i):
         pass_on(i)
@@ -218,11 +224,10 @@
     def second(i):
         arrived(1, i)
         forward(i, 1, 1)
-        some(RING - LATE + i)
+        loop(27 + (9 * i) // 2, 27 + (9 * i + 9) // 2, tell)
         unfolded(i, 1)
 
     loop(0, LATE, second)
-    loop(RING * TELL, CHIPS - 1, tell)
 
     def third_up(i):
         arrived(2, i)

time: 66.6 us -> 66.1 us (level)
  no operation moved by 1% of the time
where the time goes in v5:
time: 66.1 us; the launch traced here: 65.9 us
  Pallas kernels  60.4 us (91%)
  local copies, waits for them, and re-layouts  4.84 us (7%)
    pallas_call x1, Pallas kernels, body(): pl.pallas_call(kernel, out_shape=(jax.ShapeDtypeStruct(traces.shape, F32)...  60.4 us
    unnamed x12, local copies, waits for them, and re-layouts  4.84 us

profile of v5, /device:TPU:1, one launch (start us, length us, event | category | flops | bytes accessed | tf_op | source)
XLA Modules:
  0.0 65.9 jit_solution(4663883026030614107)
XLA Ops:
  0.6 0.0 copy-start.3
  0.6 0.0 copy-start.4
  0.7 0.6 copy-done.3
  1.3 0.0 copy-done.4
  1.3 0.0 copy-start
  1.3 0.9 %copy-done = bf16[1024,128]{1,0:T(8,128)(2,1)S(1)} copy-done((bf16[1024,128]{1,0:T(8,128)(2,1)S(1)}, bf16[1024,128]{1,0:T(8,128)(2,1)}, u32[]{:S(2)}) %copy-start) | copy-done | bytes 262168
  2.3 0.0 copy-start.1
  2.3 0.9 %copy-done.1 = bf16[1024,128]{1,0:T(8,128)(2,1)S(1)} copy-done((bf16[1024,128]{1,0:T(8,128)(2,1)S(1)}, bf16[1024,128]{1,0:T(8,128)(2,1)}, u32[]{:S(2)}) %copy-start.1) | copy-done | bytes 262168
  3.2 0.0 copy-start.2
  3.2 0.9 %copy-done.2 = f32[320,128]{1,0:T(8,128)S(1)} copy-done((f32[320,128]{1,0:T(8,128)S(1)}, f32[320,128]{1,0:T(8,128)}, u32[]{:S(2)}) %copy-start.2) | copy-done | bytes 163864
  4.1 60.4 %shard_map.68 = (f32[320,128]{1,0:T(8,128)S(1)}, bf16[1024,128]{1,0:T(8,128)(2,1)S(1)}) custom-call(bf16[1024,128]{1,0:T(8,128)(2,1)S(1)} %copy-done, bf16[1024,128]{1,0:T(8,128)(2,1)S(1)} %copy-done.1, s32[1,128]{1,0:T(1,128)S(1)} %bitcast.2, s32[1,128]{1,0:T(1,128)S(1)} %bitcast.3, f32[320,128]{1,0:T(8,128)S(1)} %copy-done.2), custom_call_target="tpu_custom_call" | custom-call | tf_op jit(solution)/shard_map/pallas_call | solution.py:437
  64.5 0.7 %copy.9 = f32[320,128]{1,0:T(8,128)} copy(f32[320,128]{1,0:T(8,128)S(1)} %get-tuple-element.4) | data formatting | bytes 327680
  65.2 0.7 %copy.10 = bf16[1024,128]{1,0:T(8,128)(2,1)} copy(bf16[1024,128]{1,0:T(8,128)(2,1)S(1)} %get-tuple-element.5) | data formatting | bytes 524288
Async XLA Ops:
  0.6 0.7 copy-start.3
  0.6 0.7 %copy-start.4 = (s32[128]{0:T(128)S(1)}, s32[128]{0:T(128)}, u32[]{:S(2)}) copy-start(s32[128]{0:T(128)} %param.8) | copy-start | bytes 1540
  1.3 0.9 %copy-start = (bf16[1024,128]{1,0:T(8,128)(2,1)S(1)}, bf16[1024,128]{1,0:T(8,128)(2,1)}, u32[]{:S(2)}) copy-start(bf16[1024,128]{1,0:T(8,128)(2,1)} %rec_hbm.1) | copy-start | bytes 786436
  2.3 0.9 %copy-start.1 = (bf16[1024,128]{1,0:T(8,128)(2,1)S(1)}, bf16[1024,128]{1,0:T(8,128)(2,1)}, u32[]{:S(2)}) copy-start(bf16[1024,128]{1,0:T(8,128)(2,1)} %foot_hbm.1) | copy-start | bytes 786436
  3.2 0.9 %copy-start.2 = (f32[320,128]{1,0:T(8,128)S(1)}, f32[320,128]{1,0:T(8,128)}, u32[]{:S(2)}) copy-start(f32[320,128]{1,0:T(8,128)} %traces_hbm.1) | copy-start | bytes 491524

commit v6 on v5

--- a/solution.py
+++ b/solution.py
@@ -354,21 +354,20 @@
             back[pl.ds(32 * g + f, 8, stride=4), :] = gathered(f, g)
     s_buf[...] = jnp.transpose(table[...])
     back[pl.ds(2, CHIPS, stride=4), :] = s_buf[pl.ds(pl.multiple_of(c * CHIPS, CHIPS), CHIPS), :]
-    back[pl.ds(3, CHIPS, stride=4), :] = jnp.zeros((CHIPS, K), F32)
 
     away = [(rz, ry) for rz in range(RING) for ry in range(RING) if rz or ry]
     for rz, ry in sorted(away, key=lambda r: -min(r[0], RING - r[0]) - min(r[1], RING - r[1])):
         p = lax.rem(zc + rz, RING) * RING + lax.rem(yc + ry, RING)
         remote(
-            back.at[pl.ds(pl.multiple_of(p * 4, 4), 4)],
-            back_in.at[pl.ds(pl.multiple_of(q * 4, 4), 4)],
+            back.at[pl.ds(pl.multiple_of(p * 4, 4), 3)],
+            back_in.at[pl.ds(pl.multiple_of(q * 4, 4), 3)],
             back_send, back_recv, p * 2 + c, x,
         ).start()
-    mine = pl.ds(pl.multiple_of(q * 4, 4), 4)
+    mine = pl.ds(pl.multiple_of(q * 4, 4), 3)
     own_back = pltpu.make_async_copy(back.at[mine], back_in.at[mine], here_sem.at[1])
     own_back.start()
     own_back.wait()
-    drain(back_in.at[pl.ds(0, (CHIPS - 1) * 4)], back_recv)
+    drain(back_in.at[pl.ds(0, (CHIPS - 1) * 3)], back_recv)
 
     slot_traces = jnp.concatenate([back_in[pl.ds(0, CHIPS, stride=4), :], back_in[pl.ds(1, CHIPS, stride=4), :]], axis=0)
     hi, lo = split(slot_traces)
@@ -428,7 +427,7 @@
 
     drain(packed.at[pl.ds(0, CHIPS - 1)], gram_send)
     drain(msg.at[pl.ds(0, (CHIPS - 1) * SENT)], msg_send)
-    drain(back.at[pl.ds(0, (CHIPS - 1) * 4)], back_send)
+    drain(back.at[pl.ds(0, (CHIPS - 1) * 3)], back_send)
 
 
 def body(recording, footprints, slot_owner, slot_pick, traces):

time: 66.1 us -> 66.1 us (level)
  no operation moved by 1% of the time
where the time goes in v6:
time: 66.1 us; the launch traced here: 65.9 us
  Pallas kernels  60.4 us (91%)
  local copies, waits for them, and re-layouts  4.84 us (7%)
    pallas_call x1, Pallas kernels, body(): pl.pallas_call(kernel, out_shape=(jax.ShapeDtypeStruct(traces.shape, F32)...  60.4 us
    unnamed x12, local copies, waits for them, and re-layouts  4.84 us

profile of v6, /device:TPU:1, one launch (start us, length us, event | category | flops | bytes accessed | tf_op | source)
XLA Modules:
  0.0 65.9 jit_solution(7031890510971168741)
XLA Ops:
  0.6 0.0 copy-start.3
  0.6 0.0 copy-start.4
  0.7 0.6 copy-done.3
  1.3 0.0 copy-done.4
  1.3 0.0 copy-start
  1.3 0.9 %copy-done = bf16[1024,128]{1,0:T(8,128)(2,1)S(1)} copy-done((bf16[1024,128]{1,0:T(8,128)(2,1)S(1)}, bf16[1024,128]{1,0:T(8,128)(2,1)}, u32[]{:S(2)}) %copy-start) | copy-done | bytes 262168
  2.3 0.0 copy-start.1
  2.3 0.9 %copy-done.1 = bf16[1024,128]{1,0:T(8,128)(2,1)S(1)} copy-done((bf16[1024,128]{1,0:T(8,128)(2,1)S(1)}, bf16[1024,128]{1,0:T(8,128)(2,1)}, u32[]{:S(2)}) %copy-start.1) | copy-done | bytes 262168
  3.2 0.0 copy-start.2
  3.2 0.9 %copy-done.2 = f32[320,128]{1,0:T(8,128)S(1)} copy-done((f32[320,128]{1,0:T(8,128)S(1)}, f32[320,128]{1,0:T(8,128)}, u32[]{:S(2)}) %copy-start.2) | copy-done | bytes 163864
  4.1 60.4 %shard_map.68 = (f32[320,128]{1,0:T(8,128)S(1)}, bf16[1024,128]{1,0:T(8,128)(2,1)S(1)}) custom-call(bf16[1024,128]{1,0:T(8,128)(2,1)S(1)} %copy-done, bf16[1024,128]{1,0:T(8,128)(2,1)S(1)} %copy-done.1, s32[1,128]{1,0:T(1,128)S(1)} %bitcast.2, s32[1,128]{1,0:T(1,128)S(1)} %bitcast.3, f32[320,128]{1,0:T(8,128)S(1)} %copy-done.2), custom_call_target="tpu_custom_call" | custom-call | tf_op jit(solution)/shard_map/pallas_call | solution.py:436
  64.5 0.7 %copy.9 = f32[320,128]{1,0:T(8,128)} copy(f32[320,128]{1,0:T(8,128)S(1)} %get-tuple-element.4) | data formatting | bytes 327680
  65.2 0.7 %copy.10 = bf16[1024,128]{1,0:T(8,128)(2,1)} copy(bf16[1024,128]{1,0:T(8,128)(2,1)S(1)} %get-tuple-element.5) | data formatting | bytes 524288
Async XLA Ops:
  0.6 0.7 copy-start.3
  0.6 0.7 %copy-start.4 = (s32[128]{0:T(128)S(1)}, s32[128]{0:T(128)}, u32[]{:S(2)}) copy-start(s32[128]{0:T(128)} %param.8) | copy-start | bytes 1540
  1.3 0.9 %copy-start = (bf16[1024,128]{1,0:T(8,128)(2,1)S(1)}, bf16[1024,128]{1,0:T(8,128)(2,1)}, u32[]{:S(2)}) copy-start(bf16[1024,128]{1,0:T(8,128)(2,1)} %rec_hbm.1) | copy-start | bytes 786436
  2.3 0.9 %copy-start.1 = (bf16[1024,128]{1,0:T(8,128)(2,1)S(1)}, bf16[1024,128]{1,0:T(8,128)(2,1)}, u32[]{:S(2)}) copy-start(bf16[1024,128]{1,0:T(8,128)(2,1)} %foot_hbm.1) | copy-start | bytes 786436
  3.2 0.9 %copy-start.2 = (f32[320,128]{1,0:T(8,128)S(1)}, f32[320,128]{1,0:T(8,128)}, u32[]{:S(2)}) copy-start(f32[320,128]{1,0:T(8,128)} %traces_hbm.1) | copy-start | bytes 491524
